TPU v7x, 128 devices: a whole 4x4x4 slice. The times are simulated.
128 devices in a mesh: gx: 8 (over y, core), gy: 16 (over x, z).
Axes of the slice: x: 4, y: 4, z: 4, core: 2. Of those that a mesh axis runs over, the one named last changes fastest.
Arguments:
- fine_rhs: float32 [131072], P(('gx', 'gy')), may hold values from -30 to 30
- fine_diagonal: float32 [131072], P(('gx', 'gy')), may hold values from 0.25 to 2
- fine_support: int32 [27, 131072], P(None, ('gx', 'gy')), may hold values from -1 to 2048, as said below
- fine_weights: float32 [27, 131072], P(None, ('gx', 'gy')), may hold values from -0.2 to 0.2
- point_inputs: bfloat16 [32, 524288], P(None, ('gx', 'gy')), may hold values from -6 to 6
- point_offsets: float32 [3, 524288], P(None, ('gx', 'gy')), may hold values from 0 to 1
- point_counts: int32 [32768], P(('gx', 'gy')), may hold values from 0 to 16
- coarse_features: bfloat16 [32, 32768], P(None, ('gx', 'gy')), may hold values from -6 to 6
- coarse_support: int32 [27, 32768], P(None, ('gx', 'gy')), may hold values from -1 to 767, as said below
- w_first: bfloat16 [32, 64], replicated, may hold values from -1 to 1
- w_second: bfloat16 [64, 32], replicated, may hold values from -0.75 to 0.75
Outputs:
- solution_fine: float32 [131072], P(('gx', 'gy'))
- residual_fine: float32 [131072], P(('gx', 'gy'))
- gram: bfloat16 [27, 27, 32768], P(None, None, ('gx', 'gy'))
Inputs may be any that keep to these rules, and one draw needn't show every extreme that they name: `fine_support`: every live entry of column u names a fine voxel u + value - 1024 inside the grid. `coarse_support`: every live entry of column v names a coarse voxel of the block just before v's block, v's own or the one just after (256 voxels a block), inside the grid.
All inputs are finite; a program needn't handle non-finite values.
Results may differ from a plain program's by a relative error of at most 0.0054.
Values may be sent and summed in bfloat16 or wider, within the bound.
A program may use at most 64 MiB of HBM per device.

v0:
```python
import jax
import jax.numpy as jnp
from jax import lax
from jax.sharding import PartitionSpec as P

SLOTS = 16
WIDTH = 32
SUPPORT = 27
ITERS = 2
REACH = 1024


def padded(shard, sides, width):
    for axis, dim in sides:
        size, length = (lax.axis_size(axis), shard.shape[dim])
        up = [(i, (i + 1) % size) for i in range(size - 1)]
        down = [(j, i) for i, j in up]
        last = lax.slice_in_dim(shard, length - width, length, axis=dim)
        leading = lax.slice_in_dim(shard, 0, width, axis=dim)
        before = lax.ppermute(last, axis, up)
        after = lax.ppermute(leading, axis, down)
        shard = jnp.concatenate([before, shard, after], axis=dim)
    return shard


def on_device(
    fine_rhs,
    fine_diagonal,
    fine_support,
    fine_weights,
    point_inputs,
    point_offsets,
    point_counts,
    coarse_features,
    coarse_support,
    w_first,
    w_second,
):
    fine_len = fine_rhs.shape[0]
    reach = REACH
    valid = fine_support >= 0
    column = jnp.arange(fine_len, dtype=jnp.int32)
    local = jnp.clip(column[None, :] + fine_support, 0, fine_len + 2 * reach - 1)
    flat_local = local.reshape(-1)
    live_w = jnp.where(valid, fine_weights, jnp.zeros_like(fine_weights))
    row_abs = jnp.sum(jnp.abs(live_w), axis=0)

    def spread_terms(terms):
        return jnp.zeros((fine_len + 2 * reach,), jnp.float32).at[flat_local].add(terms.reshape(-1))

    def combine_back(spread, from_lower, from_upper):
        middle = spread[reach : reach + fine_len]
        middle = middle.at[:reach].add(from_lower)
        return middle.at[fine_len - reach :].add(from_upper)

    def returned_part(terms):
        spread = spread_terms(terms)
        outer = jnp.concatenate([spread[:reach], spread[reach + fine_len :]])
        arrived = padded(outer, ((("gx", "gy"), 0),), 2 * reach)
        return combine_back(spread, arrived[reach : 2 * reach], arrived[4 * reach : 5 * reach])

    col_abs = returned_part(jnp.abs(live_w))
    shift = fine_diagonal + row_abs + col_abs
    solution_fine = jnp.zeros_like(fine_rhs)
    residual_fine = fine_rhs

    def squares(vec):
        return lax.psum(jnp.sum(vec * vec), ("gx", "gy"))

    direction = fine_rhs
    norm_now = squares(residual_fine)
    for step in range(ITERS):
        wide = padded(direction, ((("gx", "gy"), 0),), reach)
        backward = returned_part(live_w * direction[None, :])
        forward = jnp.sum(live_w * wide[local], axis=0)
        image = shift * direction + forward + backward
        alpha = norm_now / lax.psum(jnp.sum(direction * image), ("gx", "gy"))
        solution_fine = solution_fine + alpha * direction
        residual_fine = residual_fine - alpha * image
        norm_next = squares(residual_fine)
        direction = residual_fine + norm_next / norm_now * direction
        norm_now = norm_next
    coarse_len = point_counts.shape[0]
    rim_feats = padded(coarse_features, ((("gx", "gy"), 1),), coarse_len)
    point_hidden = jax.nn.relu(
        jnp.einsum("ei,ep->ip", w_first, point_inputs, preferred_element_type=jnp.float32)
    ).astype(jnp.bfloat16)
    point_feats = jnp.einsum(
        "ie,ip->ep", w_second, point_hidden, preferred_element_type=jnp.float32
    ).astype(jnp.bfloat16)
    feats = point_feats.reshape(WIDTH, SLOTS, coarse_len)
    offsets = point_offsets.reshape(3, SLOTS, coarse_len)
    live = (jnp.arange(SLOTS, dtype=jnp.int32)[:, None] < point_counts[None, :]).astype(jnp.float32)
    basis = jnp.stack(
        [0.5 * (1.0 - offsets) ** 2, 0.5 + offsets - offsets * offsets, 0.5 * offsets * offsets]
    )
    scale = WIDTH ** (-0.5)

    def one_entry(args):
        index, place = args
        entry_valid = (index >= 0).astype(jnp.float32)
        where_local = jnp.clip(index, 0, 3 * coarse_len - 1)
        near = rim_feats[:, where_local]
        dots = jnp.einsum("esc,ec->sc", feats, near, preferred_element_type=jnp.float32)
        bezier = basis[place // 9, 0] * basis[place // 3 % 3, 1] * basis[place % 3, 2]
        return dots * scale * bezier * live * entry_valid[None, :]

    kernel = lax.map(one_entry, (coarse_support, jnp.arange(SUPPORT, dtype=jnp.int32)))

    def one_row(row):
        return jnp.sum(row[None] * kernel, axis=1).astype(jnp.bfloat16)

    gram = lax.map(one_row, kernel)
    return (solution_fine, residual_fine, gram)


def solution(mesh):
    placed = (
        P(("gx", "gy")),
        P(("gx", "gy")),
        P(None, ("gx", "gy")),
        P(None, ("gx", "gy")),
        P(None, ("gx", "gy")),
        P(None, ("gx", "gy")),
        P(("gx", "gy")),
        P(None, ("gx", "gy")),
        P(None, ("gx", "gy")),
        P(),
        P(),
    )
    return jax.shard_map(
        on_device,
        mesh=mesh,
        in_specs=placed,
        out_specs=(P(("gx", "gy")), P(("gx", "gy")), P(None, None, ("gx", "gy"))),
        check_vma=False,
    )
```

profile of v0, /device:TPU:1, one launch (start us, length us, event | category | flops | bytes accessed | tf_op | source)
XLA Modules:
  0.0 1197.8 jit_solution(5315346654392219067)
XLA Ops:
  0.7 4.5 collective-permute-start.2
  5.2 6.8 collective-permute-start.3
  12.0 0.9 compare_select_fusion.2
  13.3 144.5 %scatter_custom_fusion = f32[3072]{0:T(1024)S(1)} fusion(s32[27648]{0:T(1024)S(1)} %bitcast.84, f32[27648]{0:T(1024)S(1)} %reshape.340, f32[]{:T(128)} %constant.290.clone.1), kind=kCustom, calls=%fused_computation.51 | custom fusion | flops 27648 | bytes 12292 | tf_op jit(solution)/shard_map/scatter-add | solution.py:49
  157.8 1.9 collective-permute-start
  159.7 7.0 collective-permute-start.1
  166.7 1.9 collective-permute-start.10
  169.4 152.4 %gather_fusion.1 = f32[27648]{0:T(1024)S(1)} fusion(f32[3072]{0:T(1024)S(1)} %pad_maximum_fusion.2, s32[27648]{0:T(1024)S(1)} %broadcast_clamp_fusion), kind=kCustom, calls=%fused_computation.1 | custom fusion | bytes 331776 | tf_op jit(solution)/shard_map/gather | solution.py:75
  321.9 144.5 %scatter_custom_fusion.1 = f32[3072]{0:T(1024)S(1)} fusion(s32[27648]{0:T(1024)S(1)} %bitcast.85, f32[27648]{0:T(1024)S(1)} %reshape.348, f32[]{:T(128)} %constant.290.clone.1), kind=kCustom, calls=%fused_computation.49 | custom fusion | flops 27648 | bytes 12292 | tf_op jit(solution)/shard_map/scatter-add | solution.py:49
  466.5 1.9 collective-permute-start.4
  468.4 7.1 collective-permute-start.5
  476.0 4.1 collective-permute-start.11
  480.7 68.5 %all-reduce = (f32[]{:T(128)}, f32[]{:T(128)}) all-reduce(f32[]{:T(128)} %get-tuple-element.307, f32[]{:T(128)} %get-tuple-element.306), channel_id=1, replica_groups=mesh['gx'=8,'gy'=16] {'gx','gy'}, use_global_device_ids=true, to_apply=%region_1.2 | all-reduce | flops 2 | bytes 16 | tf_op jit(solution)/shard_map/psum | solution.py:68
  551.1 62.6 %psum.30 = f32[]{:T(128)} all-reduce(f32[]{:T(128)} %multiply_reduce_fusion.5), channel_id=1, replica_groups=mesh['gx'=8,'gy'=16] {'gx','gy'}, use_global_device_ids=true, to_apply=%region_9.10 | all-reduce | flops 1 | bytes 8 | tf_op jit(solution)/shard_map/psum | solution.py:68
  615.1 2.8 collective-permute-start.6
  617.9 6.1 collective-permute-start.7
  624.7 152.4 %gather_fusion.2 = f32[27648]{0:T(1024)S(1)} fusion(f32[3072]{0:T(1024)S(1)} %pad_maximum_fusion.3, s32[27648]{0:T(1024)S(1)} %broadcast_clamp_fusion), kind=kCustom, calls=%fused_computation.2 | custom fusion | bytes 331776 | tf_op jit(solution)/shard_map/gather | solution.py:75
  777.2 144.5 %scatter_custom_fusion.2 = f32[3072]{0:T(1024)S(1)} fusion(s32[27648]{0:T(1024)S(1)} %bitcast.86, f32[27648]{0:T(1024)S(1)} %reshape.356, f32[]{:T(128)} %constant.290.clone.1), kind=kCustom, calls=%fused_computation.47 | custom fusion | flops 27648 | bytes 12292 | tf_op jit(solution)/shard_map/scatter-add | solution.py:49
  921.7 1.9 collective-permute-start.8
  923.7 7.6 collective-permute-start.9
  932.2 180.0 %while.37 = (s32[]{:T(128)}, f32[27,16,256]{2,1,0:T(8,128)S(1)}, s32[27,256]{1,0:T(8,128)}, bf16[32,768]{0,1:T(8,128)(2,1)S(1)}, bf16[32,16,256]{2,1,0:T(8,128)(...) while((s32[]{:T(128)}, f32[27,16,256]{2,1,0:T(8,128)S(1)}, ...), condition=%wide.region_15.16_spmd.clone, body=%wide.region_14.15_spmd.clone.sunk | while | flops 420387 | bytes 487945 | solution.py:108
  1070.4 0.9 gather_fusion
  1112.1 19.2 %while.36 = (s32[]{:T(128)}, bf16[27,27,256]{2,1,0:T(8,128)(2,1)}, f32[27,16,256]{2,1,0:T(8,128)S(1)}, s32[]{:T(128)}) while((s32[]{:T(128)}, bf16[27,27,256]{2,1,0:T(8,128)(2,1)}, f32[27,16,256]{2,1,0:T(8,128)S(1)}, s32[]{:T(128)}) %tuple.110), condition=%wide.region_18.19_spmd, body=%wide.region_16.18_spmd.sunk | while | flops 214274 | bytes 536121 | solution.py:113
  1131.9 63.9 %psum.31 = f32[]{:T(128)} all-reduce(f32[]{:T(128)} %get-tuple-element.332), channel_id=1, replica_groups=mesh['gx'=8,'gy'=16] {'gx','gy'}, use_global_device_ids=true, to_apply=%region_13.14 | all-reduce | flops 1 | bytes 8 | tf_op jit(solution)/shard_map/psum | solution.py:77
  (362 shorter events, 108.2 us)
Async XLA Ops:
  0.6 474.8 %copy-start = (bf16[32,4096]{1,0:T(8,128)(2,1)S(1)}, bf16[32,4096]{1,0:T(8,128)(2,1)}, u32[]{:S(2)}) copy-start(bf16[32,4096]{1,0:T(8,128)(2,1)} %param.43) | copy-start | bytes 786436
  0.6 12.3 %copy-start.1 = (s32[27,1024]{1,0:T(8,128)S(1)}, s32[27,1024]{1,0:T(8,128)}, u32[]{:S(2)}) copy-start(s32[27,1024]{1,0:T(8,128)} %param.41) | copy-start | bytes 331780
  0.7 12.3 %copy-start.3 = (f32[27,1024]{1,0:T(8,128)S(1)}, f32[27,1024]{1,0:T(8,128)}, u32[]{:S(2)}) copy-start(f32[27,1024]{1,0:T(8,128)} %param.42) | copy-start | bytes 331780
  0.7 168.1 %collective-permute-start.2 = (f32[1024]{0:T(1024)}, f32[1024]{0:T(1024)S(1)}, u32[]{:S(2)}, u32[]{:S(2)}) collective-permute-start(f32[1024]{0:T(1024)} %param.39), channel_id=1, source_target_pairs={{0,1},{1,2},{2,3},{3,4},{4,5},{5,6},{6,7},{7,8},{8,9},{9,10},{10,1... | collective-permute-start | bytes 12296 | tf_op jit(solution)/shard_map/ppermute | solution.py:20
  5.2 163.6 %collective-permute-start.3 = (f32[1024]{0:T(1024)}, f32[1024]{0:T(1024)S(1)}, u32[]{:S(2)}, u32[]{:S(2)}) collective-permute-start(f32[1024]{0:T(1024)} %param.39), channel_id=1, source_target_pairs={{1,0},{2,1},{3,2},{4,3},{5,4},{6,5},{7,6},{8,7},{9,8},{10,9},{11,1... | collective-permute-start | bytes 12296 | tf_op jit(solution)/shard_map/ppermute | solution.py:21
  157.8 8.9 copy-start.6
  157.8 318.1 %collective-permute-start = (f32[2048]{0:T(1024)S(1)}, f32[2048]{0:T(1024)S(1)}, u32[]{:S(2)}, u32[]{:S(2)}) collective-permute-start(f32[2048]{0:T(1024)S(1)} %pad_maximum_fusion.4), channel_id=1, source_target_pairs={{0,1},{1,2},{2,3},{3,4},{4,5},{5,6},{6,7},{7,8},{8,9},{9,10},{10,1... | collective-permute-start | bytes 24584 | tf_op jit(solution)/shard_map/ppermute | solution.py:20
  159.7 320.3 %collective-permute-start.1 = (f32[2048]{0:T(1024)S(1)}, f32[2048]{0:T(1024)S(1)}, u32[]{:S(2)}, u32[]{:S(2)}) collective-permute-start(f32[2048]{0:T(1024)S(1)} %pad_maximum_fusion.4), channel_id=1, source_target_pairs={{1,0},{2,1},{3,2},{4,3},{5,4},{6,5},{7,6},{8,7},{9,8},{10,9},{11,1... | collective-permute-start | bytes 24584 | tf_op jit(solution)/shard_map/ppermute | solution.py:21
  166.7 764.6 %collective-permute-start.10 = (bf16[32,256]{1,0:T(8,128)(2,1)S(1)}, bf16[32,256]{1,0:T(8,128)(2,1)S(1)}, u32[]{:S(2)}, u32[]{:S(2)}) collective-permute-start(bf16[32,256]{1,0:T(8,128)(2,1)S(1)} %copy-done.6), channel_id=1, source_target_pairs={{0,1},{1,2},{2,3},{3,4},{4,5},{5,6},{6,7},{7,8},{8,9},{9,10},{10,1... | collective-permute-start | bytes 49160 | tf_op jit(solution)/shard_map/ppermute | solution.py:20
  168.7 0.7 copy-start.2
  466.4 9.0 copy-start.7
  466.4 9.0 copy-start.8
  466.5 13.6 %collective-permute-start.4 = (f32[2048]{0:T(1024)S(1)}, f32[2048]{0:T(1024)S(1)}, u32[]{:S(2)}, u32[]{:S(2)}) collective-permute-start(f32[2048]{0:T(1024)S(1)} %pad_maximum_fusion.5), channel_id=1, source_target_pairs={{0,1},{1,2},{2,3},{3,4},{4,5},{5,6},{6,7},{7,8},{8,9},{9,10},{10,1... | collective-permute-start | bytes 24584 | tf_op jit(solution)/shard_map/ppermute | solution.py:20
  468.4 11.6 collective-permute-start.5
  475.5 4.6 copy-start.9
  475.9 75.2 %copy-start.4 = (f32[3,4096]{1,0:T(4,128)S(1)}, f32[3,4096]{1,0:T(4,128)}, u32[]{:S(2)}) copy-start(f32[3,4096]{1,0:T(4,128)} %param.44) | copy-start | bytes 147460
  476.0 455.3 %collective-permute-start.11 = (bf16[32,256]{1,0:T(8,128)(2,1)S(1)}, bf16[32,256]{1,0:T(8,128)(2,1)S(1)}, u32[]{:S(2)}, u32[]{:S(2)}) collective-permute-start(bf16[32,256]{1,0:T(8,128)(2,1)S(1)} %copy-done.6), channel_id=1, source_target_pairs={{1,0},{2,1},{3,2},{4,3},{5,4},{6,5},{7,6},{8,7},{9,8},{10,9},{11,1... | collective-permute-start | bytes 49160 | tf_op jit(solution)/shard_map/ppermute | solution.py:21
  615.1 9.0 collective-permute-start.6
  617.9 6.8 collective-permute-start.7
  921.7 209.6 %collective-permute-start.8 = (f32[2048]{0:T(1024)S(1)}, f32[2048]{0:T(1024)S(1)}, u32[]{:S(2)}, u32[]{:S(2)}) collective-permute-start(f32[2048]{0:T(1024)S(1)} %pad_maximum_fusion.6), channel_id=1, source_target_pairs={{0,1},{1,2},{2,3},{3,4},{4,5},{5,6},{6,7},{7,8},{8,9},{9,10},{10,1... | collective-permute-start | bytes 24584 | tf_op jit(solution)/shard_map/ppermute | solution.py:20
  923.7 207.6 %collective-permute-start.9 = (f32[2048]{0:T(1024)S(1)}, f32[2048]{0:T(1024)S(1)}, u32[]{:S(2)}, u32[]{:S(2)}) collective-permute-start(f32[2048]{0:T(1024)S(1)} %pad_maximum_fusion.6), channel_id=1, source_target_pairs={{1,0},{2,1},{3,2},{4,3},{5,4},{6,5},{7,6},{8,7},{9,8},{10,9},{11,1... | collective-permute-start | bytes 24584 | tf_op jit(solution)/shard_map/ppermute | solution.py:21
  931.5 0.7 copy-start.5
where the time goes:
time: 1200 us
  other arithmetic  481 us (40%)
  local copies, waits for them, and re-layouts  366 us (30%)
  blocking collectives  195 us (16%)
  loops' own time  95.7 us (8%)
  starting transfers between devices  53.5 us (4%)
    scatter-add x3, other arithmetic, spread_terms(): jnp.zeros((fine_len + 2 * reach,), jnp.float32).at[flat_local]  434 us
    gather x4, local copies, waits for them, and re-layouts, on_device(): forward = jnp.sum(live_w * wide[local], axis=0)  305 us
    psum x2, blocking collectives, squares(): return lax.psum(jnp.sum(vec * vec), ('gx', 'gy'))  131 us
    another operation x1, loops' own time, on_device(): lax.map(one_entry, (coarse_support, jnp.arange(SUPPORT, dtype=jnp.int32)))  95.7 us
    psum x1, blocking collectives, on_device(): alpha = norm_now / lax.psum(jnp.sum(direction * image), ('gx', 'gy'))  63.9 us
    ppermute x6, starting transfers between devices, padded(): after = lax.ppermute(leading, axis, down)  38.5 us
  transfers between devices with their start and end apart: 12, of which 1 were waited for; matrix products, arithmetic and copies ran while one was open for 71% of the time, Pallas kernels for 0%

commit v1 on v0

v1 whole, which is shorter than its diff:
```python
import functools

import jax
import jax.numpy as jnp
from jax import lax
from jax.experimental import pallas as pl
from jax.experimental.pallas import tpu as pltpu
from jax.sharding import PartitionSpec as P

MESH = pl.DeviceIdType.MESH
F32 = jnp.float32
BF16 = jnp.bfloat16
SUPPORT = 27
LANES = 128
ROWS = 8
CLASSES = 17
WINDOW = 24
SLOTS = 16
WIDTH = 32
HIDDEN = 64
COARSE = 256
POINTS = 4096
NT = (((1,), (1,)), ((), ()))
TN = (((0,), (0,)), ((), ()))


def spread_rows(row, shape):
    return jnp.broadcast_to(row, shape)


def kernel(
    n_gx,
    n_gy,
    rhs, rhs_row, diag, sup, wts, pin, off, cnt, cf, cs, w1, w2,
    sol_o, res_o, gram_o,
    row0, diag_v, sup_v, wts_v, pin_v, off_v, cnt_v, cs_v, w1_v, w2_v,
    hi_s, lo_s, lw_s, xw0, xw1, row1, fwd, quad, rabs, q0_s, shift_s, sol_v, res_v, mid0, mid1,
    sp_out0, sp_in0, sp_out1, sp_in1,
    ag, agx,
    cfw, fwin, feats, near, kern, gram_v,
    in_sem, halo_send, halo_recv, cf_send, cf_recv, sp_send, sp_recv,
    ag_send, ag_recv, agx_send, agx_recv, out_sem,
):
    gx = lax.axis_index("gx")
    gy = lax.axis_index("gy")
    n = n_gx * n_gy
    block = gx * n_gy + gy
    right_b = lax.rem(block + 1, n)
    left_b = lax.rem(block + n - 1, n)
    right = (lax.div(right_b, n_gy), lax.rem(right_b, n_gy))
    left = (lax.div(left_b, n_gy), lax.rem(left_b, n_gy))

    moves = [
        (sup, sup_v), (wts, wts_v), (rhs, xw0.at[pl.ds(8, 8)]), (rhs_row, row0), (cf, cfw.at[1]), (diag, diag_v),
        (pin, pin_v), (w1, w1_v), (w2, w2_v), (cs, cs_v), (off, off_v), (cnt, cnt_v),
    ]
    copies = [pltpu.make_async_copy(src, dst, in_sem.at[i]) for i, (src, dst) in enumerate(moves)]
    for copy in copies:
        copy.start()

    barrier = pltpu.get_barrier_semaphore()
    pl.semaphore_signal(barrier, inc=1, device_id=left, device_id_type=MESH)
    pl.semaphore_signal(barrier, inc=1, device_id=right, device_id_type=MESH)
    for d in range(1, n_gy):
        pl.semaphore_signal(barrier, inc=1, device_id=(gx, lax.rem(gy + d, n_gy)), device_id_type=MESH)
    for d in range(1, n_gx):
        pl.semaphore_signal(barrier, inc=1, device_id=(lax.rem(gx + d, n_gx), gy), device_id_type=MESH)

    def remote(src, dst, send, recv, device):
        return pltpu.make_async_remote_copy(
            src_ref=src, dst_ref=dst, send_sem=send, recv_sem=recv, device_id=device, device_id_type=MESH
        )

    copies[0].wait()
    copies[1].wait()
    lane = lax.broadcasted_iota(jnp.int32, (8, LANES), 1)
    for b in range(4):
        rows = 8 if b < 3 else 3
        for r in range(ROWS):
            at = (slice(8 * b, 8 * b + rows), slice(LANES * r, LANES * (r + 1)))
            value = sup_v[at]
            place = value + lane[:rows]
            live = jnp.where(value >= 0, wts_v[at], 0.0)
            hi = lax.shift_right_arithmetic(place, 7)
            lo = jnp.bitwise_and(place, 127)
            if rows < 8:
                pad = 8 - rows
                at = (slice(8 * b, 8 * b + 8), at[1])
                hi = jnp.concatenate([hi, jnp.full((pad, LANES), -1, jnp.int32)], axis=0)
                lo = jnp.concatenate([lo, jnp.zeros((pad, LANES), jnp.int32)], axis=0)
                live = jnp.concatenate([live, jnp.zeros((pad, LANES), F32)], axis=0)
            hi_s[at] = hi
            lo_s[at] = lo
            lw_s[at] = live

    for i in (2, 3, 4, 5):
        copies[i].wait()
    pl.semaphore_wait(barrier, 2 + (n_gy - 1) + (n_gx - 1))

    def halo(window, k):
        return [
            remote(window.at[pl.ds(8, 8)], window.at[pl.ds(0, 8)], halo_send.at[k, 0], halo_recv.at[k, 0], right),
            remote(window.at[pl.ds(8, 8)], window.at[pl.ds(16, 8)], halo_send.at[k, 1], halo_recv.at[k, 1], left),
        ]

    halo0 = halo(xw0, 0)
    for copy in halo0:
        copy.start()
    cf_halo = [
        remote(cfw.at[1], cfw.at[0], cf_send.at[0], cf_recv.at[0], right),
        remote(cfw.at[1], cfw.at[2], cf_send.at[1], cf_recv.at[1], left),
    ]
    for copy in cf_halo:
        copy.start()

    iota_hi = lax.broadcasted_iota(jnp.int32, (WINDOW, LANES), 0)
    iota_lo = lax.broadcasted_iota(jnp.int32, (LANES, LANES), 0)

    def two_terms(value):
        first = value.astype(BF16).astype(F32)
        return [first, value - first]

    def scatter(field_row, with_abs):
        count = 4 if with_abs else 2

        def step(j, total):
            hi = hi_s[pl.ds(j, 1), :]
            lo = lo_s[pl.ds(j, 1), :]
            w = lw_s[pl.ds(j, 1), :]
            terms = two_terms(w * field_row[...])
            if with_abs:
                terms = terms + two_terms(jnp.abs(w))
            left_parts, ones = [], []
            for r in range(ROWS):
                at = slice(LANES * r, LANES * (r + 1))
                hit = spread_rows(hi[:, at], (WINDOW, LANES)) == iota_hi - r
                left_parts.append(
                    jnp.concatenate(
                        [jnp.where(hit, spread_rows(t[:, at], (WINDOW, LANES)), 0.0) for t in terms], axis=0
                    ).astype(BF16)
                )
                ones.append(
                    jnp.where(spread_rows(lo[:, at], (LANES, LANES)) == iota_lo, 1.0, 0.0).astype(BF16)
                )
            return total + lax.dot_general(
                jnp.concatenate(left_parts, axis=1), jnp.concatenate(ones, axis=1), NT, preferred_element_type=F32
            )

        total = lax.fori_loop(0, SUPPORT, step, jnp.zeros((WINDOW * count, LANES), F32))
        out = [total[:24] + total[24:48]]
        if with_abs:
            out.append(total[48:72] + total[72:96])
        return out

    def send_spread(parts, out, into, k):
        for i, part in enumerate(parts):
            out[0, 8 * i : 8 * i + 8, :] = part[0:8]
            out[1, 8 * i : 8 * i + 8, :] = part[16:24]
        copies = [
            remote(out.at[0], into.at[0], sp_send.at[k, 0], sp_recv.at[k, 0], left),
            remote(out.at[1], into.at[1], sp_send.at[k, 1], sp_recv.at[k, 1], right),
        ]
        for copy in copies:
            copy.start()
        return copies

    def forward(window, with_abs):
        def row(r, carry):
            near_rows = [spread_rows(window[pl.ds(r + k, 1), :], (8, LANES)) for k in range(CLASSES)]
            lanes = pl.ds(pl.multiple_of(r * LANES, LANES), LANES)
            total = jnp.zeros((8, LANES), F32)
            squares = jnp.zeros((8, LANES), F32)
            weight = jnp.zeros((8, LANES), F32)
            for b in range(4):
                hi = hi_s[8 * b : 8 * b + 8, lanes]
                lo = lo_s[8 * b : 8 * b + 8, lanes]
                w = lw_s[8 * b : 8 * b + 8, lanes]
                got = jnp.zeros((8, LANES), F32)
                for k in range(CLASSES):
                    got = jnp.where(hi == k, jnp.take_along_axis(near_rows[k], lo, axis=1, mode="promise_in_bounds"), got)
                total = total + w * got
                if with_abs:
                    size = jnp.abs(w)
                    squares = squares + size * (got * got)
                    weight = weight + size
            fwd[pl.ds(r, 1), :] = jnp.sum(total, axis=0, keepdims=True)
            if with_abs:
                quad[pl.ds(r, 1), :] = jnp.sum(squares, axis=0, keepdims=True)
                rabs[pl.ds(r, 1), :] = jnp.sum(weight, axis=0, keepdims=True)
            return carry

        lax.fori_loop(0, ROWS, row, 0)

    def gather_first(k, tile):
        ag[k, gy] = tile
        copies = []
        for d in range(1, n_gy):
            copies.append(
                remote(ag.at[k, gy], ag.at[k, gy], ag_send.at[k, d], ag_recv.at[k, d], (gx, lax.rem(gy + d, n_gy)))
            )
            copies[-1].start()
        return copies

    def gather_second(k, copies):
        for copy in copies:
            copy.wait()
        agx[k, gx] = jnp.sum(ag[k], axis=0)
        copies = []
        for d in range(1, n_gx):
            copies.append(
                remote(agx.at[k, gx], agx.at[k, gx], agx_send.at[k, d], agx_recv.at[k, d], (lax.rem(gx + d, n_gx), gy))
            )
            copies[-1].start()
        return copies

    def gather_end(k, copies):
        for copy in copies:
            copy.wait()
        total = jnp.sum(jnp.sum(agx[k], axis=0), axis=1, keepdims=True)
        return total[0:1], total[1:2]

    def tile_of(first, second):
        return jnp.concatenate(
            [
                jnp.sum(first, axis=0, keepdims=True),
                jnp.sum(second, axis=0, keepdims=True),
                jnp.zeros((6, LANES), F32),
            ],
            axis=0,
        )

    def split_off(parts, out, into, k, keep):
        for i, part in enumerate(parts):
            keep[8 * i : 8 * i + 8, :] = part[8:16]
        return send_spread(parts, out, into, k)

    spread0 = split_off(scatter(row0, True), sp_out0, sp_in0, 0, mid0)
    for copy in halo0:
        copy.wait()
    forward(xw0, True)
    r0 = xw0[8:16, :]
    first0 = gather_first(
        0, tile_of(r0 * r0, (diag_v[...] + rabs[...]) * (r0 * r0) + quad[...] + 2.0 * r0 * fwd[...])
    )

    for i in range(6, 12):
        copies[i].wait()

    chunk = 512

    def mlp(i, carry):
        at = pl.ds(pl.multiple_of(i * chunk, chunk), chunk)
        hidden = lax.dot_general(w1_v[...], pin_v[:, at], TN, preferred_element_type=F32)
        hidden = jnp.maximum(hidden, 0.0).astype(BF16)
        out = lax.dot_general(w2_v[...], hidden, TN, preferred_element_type=F32)
        feats[:, at] = out.astype(BF16).astype(F32)
        return carry

    lax.fori_loop(0, POINTS // chunk, mlp, 0)
    second0 = gather_second(0, first0)

    for copy in cf_halo:
        copy.wait()
    for side in range(3):
        fwin[:, COARSE * side : COARSE * (side + 1)] = cfw[side].astype(F32)

    def support_features(e, carry):
        line = fwin[pl.ds(e, 1), :]
        sources = [spread_rows(line[:, LANES * k : LANES * (k + 1)], (8, LANES)) for k in range(6)]
        for c in range(2):
            for b in range(4):
                rows = 8 if b < 3 else 3
                value = cs_v[8 * b : 8 * b + rows, LANES * c : LANES * (c + 1)]
                if rows < 8:
                    value = jnp.concatenate([value, jnp.full((8 - rows, LANES), -1, jnp.int32)], axis=0)
                hi = lax.shift_right_arithmetic(value, 7)
                lo = jnp.bitwise_and(value, 127)
                got = jnp.zeros((8, LANES), F32)
                for k in range(6):
                    got = jnp.where(hi == k, jnp.take_along_axis(sources[k], lo, axis=1, mode="promise_in_bounds"), got)
                near[c, e, 8 * b : 8 * b + 8, :] = got
        return carry

    lax.fori_loop(0, WIDTH, support_features, 0)

    rr0, dad0 = gather_end(0, second0)
    alpha0 = rr0 / dad0
    for copy in spread0:
        copy.wait()
    shift_s[...] = diag_v[...] + rabs[...] + (mid0[8:16, :] + sp_in0[0, 8:16, :] + sp_in0[1, 8:16, :])
    q0_s[...] = shift_s[...] * r0 + fwd[...] + (mid0[0:8, :] + sp_in0[0, 0:8, :] + sp_in0[1, 0:8, :])
    r1 = r0 - alpha0 * q0_s[...]
    xw1[8:16, :] = r1
    halo1 = halo(xw1, 1)
    for copy in halo1:
        copy.start()
    for r in range(ROWS):
        row1[0:1, LANES * r : LANES * (r + 1)] = r1[r : r + 1]

    spread1 = split_off(scatter(row1, False), sp_out1, sp_in1, 1, mid1)
    for copy in halo1:
        copy.wait()
    forward(xw1, False)
    r1 = xw1[8:16, :]
    first1 = gather_first(1, tile_of(r1 * r1, shift_s[...] * (r1 * r1) + 2.0 * r1 * fwd[...]))

    iota_j = lax.broadcasted_iota(jnp.int32, (32, LANES), 0)
    digit = [lax.div(iota_j, 9), lax.rem(lax.div(iota_j, 3), 3), lax.rem(iota_j, 3)]
    group = 4

    def kernel_values(i, carry):
        c = lax.rem(i, 2)
        s0 = lax.div(i, 2) * group
        points = [pl.ds(pl.multiple_of((s0 + g) * COARSE + c * LANES, LANES), LANES) for g in range(group)]
        dots = [[jnp.zeros((8, LANES), F32) for _ in range(4)] for _ in range(group)]
        for e in range(WIDTH):
            sources = [near[c, e, 8 * b : 8 * b + 8, :] for b in range(4)]
            for g in range(group):
                feat = spread_rows(feats[e : e + 1, points[g]], (8, LANES))
                dots[g] = [dots[g][b] + feat * sources[b] for b in range(4)]
        counts = cnt_v[pl.ds(c, 1), :]
        for g in range(group):
            factor = jnp.where(s0 + g < counts, WIDTH**-0.5, 0.0)
            product = None
            for a in range(3):
                t = off_v[a : a + 1, points[g]]
                q = [0.5 * (1.0 - t) * (1.0 - t), 0.5 + t - t * t, 0.5 * t * t]
                if a == 0:
                    q = [part * factor for part in q]
                q = [spread_rows(part, (32, LANES)) for part in q]
                value = jnp.where(digit[a] == 0, q[0], jnp.where(digit[a] == 1, q[1], q[2]))
                product = value if product is None else product * value
            for b in range(4):
                kern[c, s0 + g, 8 * b : 8 * b + 8, :] = dots[g][b] * product[8 * b : 8 * b + 8]
        return carry

    lax.fori_loop(0, 2 * SLOTS // group, kernel_values, 0)
    second1 = gather_second(1, first1)

    def gram_rows(i, carry):
        c = lax.rem(i, 2)
        j0 = lax.div(i, 2) * 3
        here = pl.ds(pl.multiple_of(c * LANES, LANES), LANES)
        sums = [[jnp.zeros((8, LANES), F32) for _ in range(4)] for _ in range(3)]
        for s in range(SLOTS):
            columns = [kern[c, s, 8 * b : 8 * b + 8, :] for b in range(4)]
            for g in range(3):
                one = spread_rows(kern[c, s, pl.ds(j0 + g, 1), :], (8, LANES))
                sums[g] = [sums[g][b] + one * columns[b] for b in range(4)]
        for g in range(3):
            whole = jnp.concatenate(sums[g], axis=0).astype(BF16)
            gram_v[j0 + g, :, here] = whole[:SUPPORT]
        return carry

    lax.fori_loop(0, 18, gram_rows, 0)
    out2 = pltpu.make_async_copy(gram_v, gram_o, out_sem.at[2])
    out2.start()

    rr1, rar1 = gather_end(1, second1)
    beta = rr1 / rr0
    alpha1 = rr1 / (rar1 - beta * rr1 / alpha0)
    for copy in spread1:
        copy.wait()
    image = shift_s[...] * r1 + fwd[...] + (mid1[...] + sp_in1[0] + sp_in1[1])
    sol_v[...] = alpha0 * r0 + alpha1 * (r1 + beta * r0)
    res_v[...] = r1 - alpha1 * (image + beta * q0_s[...])
    out0 = pltpu.make_async_copy(sol_v, sol_o, out_sem.at[0])
    out1 = pltpu.make_async_copy(res_v, res_o, out_sem.at[1])
    out0.start()
    out1.start()
    out0.wait()
    out1.wait()
    out2.wait()


def on_device(n_gx, n_gy, rhs, diag, sup, wts, pin, off, cnt, cf, cs, w1, w2):
    vm = pltpu.VMEM
    dma = pltpu.SemaphoreType.DMA
    fine = (ROWS, LANES)
    sol, res, gram = pl.pallas_call(
        functools.partial(kernel, n_gx, n_gy),
        out_shape=[
            jax.ShapeDtypeStruct(fine, F32),
            jax.ShapeDtypeStruct(fine, F32),
            jax.ShapeDtypeStruct((SUPPORT, SUPPORT, COARSE), BF16),
        ],
        in_specs=[pl.BlockSpec(memory_space=pl.ANY)] * 12,
        out_specs=[pl.BlockSpec(memory_space=pl.ANY)] * 3,
        scratch_shapes=[
            vm((1, 1024), F32),
            vm(fine, F32),
            vm((SUPPORT, 1024), jnp.int32),
            vm((SUPPORT, 1024), F32),
            vm((WIDTH, POINTS), BF16),
            vm((3, POINTS), F32),
            vm((2, LANES), jnp.int32),
            vm((SUPPORT, COARSE), jnp.int32),
            vm((WIDTH, HIDDEN), BF16),
            vm((HIDDEN, WIDTH), BF16),
            vm((32, 1024), jnp.int32),
            vm((32, 1024), jnp.int32),
            vm((32, 1024), F32),
            vm((WINDOW, LANES), F32),
            vm((WINDOW, LANES), F32),
            vm((1, 1024), F32),
            vm(fine, F32),
            vm(fine, F32),
            vm(fine, F32),
            vm(fine, F32),
            vm(fine, F32),
            vm(fine, F32),
            vm(fine, F32),
            vm((16, LANES), F32),
            vm((8, LANES), F32),
            vm((2, 16, LANES), F32),
            vm((2, 16, LANES), F32),
            vm((2, 8, LANES), F32),
            vm((2, 8, LANES), F32),
            vm((2, n_gy, 8, LANES), F32),
            vm((2, n_gx, 8, LANES), F32),
            vm((3, WIDTH, COARSE), BF16),
            vm((WIDTH, 3 * COARSE), F32),
            vm((WIDTH, POINTS), F32),
            vm((2, WIDTH, 32, LANES), F32),
            vm((2, SLOTS, 32, LANES), F32),
            vm((SUPPORT, SUPPORT, COARSE), BF16),
            dma((12,)),
            dma((2, 2)),
            dma((2, 2)),
            dma((2,)),
            dma((2,)),
            dma((2, 2)),
            dma((2, 2)),
            dma((2, n_gy)),
            dma((2, n_gy)),
            dma((2, n_gx)),
            dma((2, n_gx)),
            dma((3,)),
        ],
        compiler_params=pltpu.CompilerParams(
            collective_id=0, has_side_effects=True, vmem_limit_bytes=48 * 1024 * 1024
        ),
    )(
        rhs.reshape(fine), rhs.reshape(1, 1024), diag.reshape(fine), sup, wts, pin, off,
        cnt.reshape(2, LANES), cf, cs, w1, w2,
    )
    return sol.reshape(1024), res.reshape(1024), gram


def solution(mesh):
    both = ("gx", "gy")
    placed = (
        P(both), P(both), P(None, both), P(None, both), P(None, both), P(None, both),
        P(both), P(None, both), P(None, both), P(), P(),
    )
    return jax.shard_map(
        functools.partial(on_device, mesh.shape["gx"], mesh.shape["gy"]),
        mesh=mesh,
        in_specs=placed,
        out_specs=(P(both), P(both), P(None, None, both)),
        check_vma=False,
    )
```

time: 1200 us -> 53.4 us (0.04)
  other arithmetic: 481 us -> 0 us
  local copies, waits for them, and re-layouts: 366 us -> 7.81 us
  blocking collectives: 195 us -> 0 us
  loops' own time: 95.7 us -> 0 us
  starting transfers between devices: 53.5 us -> 0 us
  Pallas kernels: 0 us -> 44.5 us
    scatter-add x3 -> x0, other arithmetic: 434 us -> none  [spread_terms(): jnp.zeros((fine_len + 2 * reach,), jnp.float32).at[flat_local]]
    gather x31 -> x0, local copies, waits for them, and re-layouts: 328 us -> none  [the longest x4 305 us: on_device(): forward = jnp.sum(live_w * wide[local], axis=0)]
    psum x3 -> x0, blocking collectives: 195 us -> none  [the longest x2 131 us: squares(): return lax.psum(jnp.sum(vec * vec), ('gx', 'gy'))]
    another operation x2 -> x0, loops' own time: 95.7 us -> none  [the longest x1 95.7 us: on_device(): lax.map(one_entry, (coarse_support, jnp.arange(SUPPORT, dtype=jnp.int32)))]
    ppermute x12 -> x0, starting transfers between devices: 53.5 us -> none  [the longest x6 38.5 us: padded(): after = lax.ppermute(leading, axis, down)]
    pallas_call x0 -> x1, Pallas kernels: none -> 44.5 us  [on_device(): pl.pallas_call(functools.partial(kernel, n_gx, n_gy), out_shape=[jax.Shap...]
    select_n x29 -> x0, other arithmetic: 20.3 us -> none  [the longest x27 19.2 us: one_entry(): near = rim_feats[:, where_local]]
    mul x28 -> x0, other arithmetic: 19.2 us -> none  [the longest x27 19.1 us: one_entry(): return dots * scale * bezier * live * entry_valid[None, :]]
  transfers between devices with their start and end apart: 12 -> 0, of which waited for: 1 -> 0; matrix products, arithmetic and copies ran while one was open for 71% -> 0% of each run, Pallas kernels for 0% -> 0%
where the time goes in v1:
time: 53.4 us; the launch traced here: 53 us
  Pallas kernels  44.5 us (83%)
  local copies, waits for them, and re-layouts  7.81 us (15%)
  between operations  0.71 us (1%)
    pallas_call x1, Pallas kernels, on_device(): pl.pallas_call(functools.partial(kernel, n_gx, n_gy), out_shape=[jax.Shap...  44.5 us
    unnamed x24, local copies, waits for them, and re-layouts  7.81 us

profile of v1, /device:TPU:1, one launch (start us, length us, event | category | flops | bytes accessed | tf_op | source)
XLA Modules:
  0.0 53.0 jit_solution(12766161705325437104)
XLA Ops:
  0.6 0.0 copy-start.6
  0.6 0.0 copy-start.5
  0.7 0.0 copy-start.7
  0.7 0.0 copy-start.9
  0.7 0.8 %copy.14.w2 = bf16[64,32]{1,0:T(8,128)(2,1)S(1)} copy(bf16[64,32]{0,1:T(8,128)(2,1)} %param.21) | data formatting | bytes 8192 | tf_op args[10]
  1.5 0.0 copy-done.6
  1.5 0.0 copy-done.5
  1.5 0.0 copy-done.7
  1.5 0.0 copy-done.9
  1.5 0.0 copy-start
  1.5 0.9 %copy-done = bf16[32,4096]{1,0:T(8,128)(2,1)S(1)} copy-done((bf16[32,4096]{1,0:T(8,128)(2,1)S(1)}, bf16[32,4096]{1,0:T(8,128)(2,1)}, u32[]{:S(2)}) %copy-start) | copy-done | bytes 262168
  2.5 0.0 copy-start.1
  2.5 0.9 %copy-done.1 = s32[27,1024]{1,0:T(8,128)S(1)} copy-done((s32[27,1024]{1,0:T(8,128)S(1)}, s32[27,1024]{1,0:T(8,128)}, u32[]{:S(2)}) %copy-start.1) | copy-done | bytes 110616
  3.4 0.9 %copy-done.2 = f32[27,1024]{1,0:T(8,128)S(1)} copy-done((f32[27,1024]{1,0:T(8,128)S(1)}, f32[27,1024]{1,0:T(8,128)}, u32[]{:S(2)}) %copy-start.2) | copy-done | bytes 110616
  4.3 0.0 copy-start.3
  4.3 0.8 %copy-done.3 = f32[3,4096]{1,0:T(4,128)S(1)} copy-done((f32[3,4096]{1,0:T(4,128)S(1)}, f32[3,4096]{1,0:T(4,128)}, u32[]{:S(2)}) %copy-start.3) | copy-done | bytes 49176
  5.1 0.0 copy-start.4
  5.1 0.8 %copy-done.4 = s32[27,256]{1,0:T(8,128)S(1)} copy-done((s32[27,256]{1,0:T(8,128)S(1)}, s32[27,256]{1,0:T(8,128)}, u32[]{:S(2)}) %copy-start.4) | copy-done | bytes 27672
  5.9 0.0 copy-start.8
  5.9 0.7 %copy-done.8 = f32[1024]{0:T(1024)S(1)} copy-done((f32[1024]{0:T(1024)S(1)}, f32[1024]{0:T(1024)}, u32[]{:S(2)}) %copy-start.8) | copy-done | bytes 4120
  6.6 44.5 %shard_map.130 = (f32[8,128]{1,0:T(8,128)S(1)}, f32[8,128]{1,0:T(8,128)S(1)}, bf16[27,27,256]{2,1,0:T(8,128)(2,1)S(1)}) custom-call(f32[8,128]{1,0:T(8,128)S(1)} %bitcast.6, f32[1,1024]{1,0:T(1,128)S(1)} %bitcast.7, f32[8,128]{1,0:T(8,128)S(1)} %bitcast.8, s32[27,1024]{1,0:T(8,128)S(1)} %copy-done.1, f32[27,1024]{1,0:T(8,128)S(1)} %copy-done.2, ...), custom_call_target="tpu_custom_call" | custom-call | tf_op jit(solution)/shard_map/pallas_call | solution.py:380
  51.1 0.6 %copy.18 = f32[1024]{0:T(1024)} copy(f32[1024]{0:T(1024)S(1)} %bitcast.10) | data formatting | bytes 8192
  51.7 0.6 %copy.19 = f32[1024]{0:T(1024)} copy(f32[1024]{0:T(1024)S(1)} %bitcast.9) | data formatting | bytes 8192
  52.3 0.8 %copy.20 = bf16[27,27,256]{2,1,0:T(8,128)(2,1)} copy(bf16[27,27,256]{2,1,0:T(8,128)(2,1)S(1)} %get-tuple-element.14) | data formatting | bytes 746496
  (1 shorter events, 0.0 us)
Async XLA Ops:
  0.6 0.9 %copy-start.6 = (bf16[32,256]{1,0:T(8,128)(2,1)S(1)}, bf16[32,256]{1,0:T(8,128)(2,1)}, u32[]{:S(2)}) copy-start(bf16[32,256]{1,0:T(8,128)(2,1)} %cf.1) | copy-start | bytes 49156
  0.6 0.8 %copy-start.5 = (f32[1024]{0:T(1024)S(1)}, f32[1024]{0:T(1024)}, u32[]{:S(2)}) copy-start(f32[1024]{0:T(1024)} %param.11) | copy-start | bytes 12292
  0.7 0.8 %copy-start.7 = (bf16[32,64]{1,0:T(8,128)(2,1)S(1)}, bf16[32,64]{1,0:T(8,128)(2,1)}, u32[]{:S(2)}) copy-start(bf16[32,64]{1,0:T(8,128)(2,1)} %w1.1) | copy-start | bytes 12292
  0.7 0.8 %copy-start.9 = (s32[256]{0:T(256)S(1)}, s32[256]{0:T(256)}, u32[]{:S(2)}) copy-start(s32[256]{0:T(256)} %param.17) | copy-start | bytes 3076
  1.5 1.0 %copy-start = (bf16[32,4096]{1,0:T(8,128)(2,1)S(1)}, bf16[32,4096]{1,0:T(8,128)(2,1)}, u32[]{:S(2)}) copy-start(bf16[32,4096]{1,0:T(8,128)(2,1)} %pin.1) | copy-start | bytes 786436
  2.5 0.9 %copy-start.1 = (s32[27,1024]{1,0:T(8,128)S(1)}, s32[27,1024]{1,0:T(8,128)}, u32[]{:S(2)}) copy-start(s32[27,1024]{1,0:T(8,128)} %sup.1) | copy-start | bytes 331780
  3.4 0.9 %copy-start.2 = (f32[27,1024]{1,0:T(8,128)S(1)}, f32[27,1024]{1,0:T(8,128)}, u32[]{:S(2)}) copy-start(f32[27,1024]{1,0:T(8,128)} %wts.1) | copy-start | bytes 331780
  4.3 0.8 %copy-start.3 = (f32[3,4096]{1,0:T(4,128)S(1)}, f32[3,4096]{1,0:T(4,128)}, u32[]{:S(2)}) copy-start(f32[3,4096]{1,0:T(4,128)} %off.1) | copy-start | bytes 147460
  5.1 0.8 %copy-start.4 = (s32[27,256]{1,0:T(8,128)S(1)}, s32[27,256]{1,0:T(8,128)}, u32[]{:S(2)}) copy-start(s32[27,256]{1,0:T(8,128)} %cs.1) | copy-start | bytes 82948
  5.9 0.7 %copy-start.8 = (f32[1024]{0:T(1024)S(1)}, f32[1024]{0:T(1024)}, u32[]{:S(2)}) copy-start(f32[1024]{0:T(1024)} %param.12) | copy-start | bytes 12292

commit v2 on v1

--- a/solution.py
+++ b/solution.py
@@ -34,24 +34,26 @@
     rhs, rhs_row, diag, sup, wts, pin, off, cnt, cf, cs, w1, w2,
     sol_o, res_o, gram_o,
     row0, diag_v, sup_v, wts_v, pin_v, off_v, cnt_v, cs_v, w1_v, w2_v,
-    hi_s, lo_s, lw_s, xw0, xw1, row1, fwd, quad, rabs, q0_s, shift_s, sol_v, res_v, mid0, mid1,
-    sp_out0, sp_in0, sp_out1, sp_in1,
+    hi_s, lo_s, lw_s, xw0, xw1, row1, fwd, rabs, shift_s, part, mid1, sol_v, res_v,
+    to_left, to_right, from_left, from_right, to_left1, to_right1, from_left1, from_right1,
     ag, agx,
     cfw, fwin, feats, near, kern, gram_v,
-    in_sem, halo_send, halo_recv, cf_send, cf_recv, sp_send, sp_recv,
+    in_sem, halo_send, halo_recv, cf_send, cf_recv, ex_send, ex_recv,
     ag_send, ag_recv, agx_send, agx_recv, out_sem,
 ):
     gx = lax.axis_index("gx")
     gy = lax.axis_index("gy")
     n = n_gx * n_gy
     block = gx * n_gy + gy
-    right_b = lax.rem(block + 1, n)
-    left_b = lax.rem(block + n - 1, n)
-    right = (lax.div(right_b, n_gy), lax.rem(right_b, n_gy))
-    left = (lax.div(left_b, n_gy), lax.rem(left_b, n_gy))
+
+    def device(step):
+        other = lax.rem(block + n + step, n)
+        return lax.div(other, n_gy), lax.rem(other, n_gy)
+
+    left2, left, right, right2 = device(-2), device(-1), device(1), device(2)
 
     moves = [
-        (sup, sup_v), (wts, wts_v), (rhs, xw0.at[pl.ds(8, 8)]), (rhs_row, row0), (cf, cfw.at[1]), (diag, diag_v),
+        (rhs, xw0.at[pl.ds(8, 8)]), (cf, cfw.at[1]), (sup, sup_v), (wts, wts_v), (rhs_row, row0), (diag, diag_v),
         (pin, pin_v), (w1, w1_v), (w2, w2_v), (cs, cs_v), (off, off_v), (cnt, cnt_v),
     ]
     copies = [pltpu.make_async_copy(src, dst, in_sem.at[i]) for i, (src, dst) in enumerate(moves)]
@@ -59,8 +61,8 @@
         copy.start()
 
     barrier = pltpu.get_barrier_semaphore()
-    pl.semaphore_signal(barrier, inc=1, device_id=left, device_id_type=MESH)
-    pl.semaphore_signal(barrier, inc=1, device_id=right, device_id_type=MESH)
+    for other in (left, right, left2, right2):
+        pl.semaphore_signal(barrier, inc=1, device_id=other, device_id_type=MESH)
     for d in range(1, n_gy):
         pl.semaphore_signal(barrier, inc=1, device_id=(gx, lax.rem(gy + d, n_gy)), device_id_type=MESH)
     for d in range(1, n_gx):
@@ -71,8 +73,32 @@
             src_ref=src, dst_ref=dst, send_sem=send, recv_sem=recv, device_id=device, device_id_type=MESH
         )
 
-    copies[0].wait()
-    copies[1].wait()
+    for i in (0, 1):
+        copies[i].wait()
+    pl.semaphore_wait(barrier, 4 + (n_gy - 1) + (n_gx - 1))
+
+    started = []
+
+    def arrive(copies):
+        for copy in copies:
+            copy.wait_recv()
+        started.extend(copies)
+
+    halo0 = [
+        remote(xw0.at[pl.ds(8, 8)], xw0.at[pl.ds(0, 8)], halo_send.at[0], halo_recv.at[0], right),
+        remote(xw0.at[pl.ds(8, 8)], xw0.at[pl.ds(16, 8)], halo_send.at[1], halo_recv.at[1], left),
+    ]
+    for copy in halo0:
+        copy.start()
+    cf_halo = [
+        remote(cfw.at[1], cfw.at[0], cf_send.at[0], cf_recv.at[0], right),
+        remote(cfw.at[1], cfw.at[2], cf_send.at[1], cf_recv.at[1], left),
+    ]
+    for copy in cf_halo:
+        copy.start()
+
+    for i in range(2, 6):
+        copies[i].wait()
     lane = lax.broadcasted_iota(jnp.int32, (8, LANES), 1)
     for b in range(4):
         rows = 8 if b < 3 else 3
@@ -92,26 +118,6 @@
             hi_s[at] = hi
             lo_s[at] = lo
             lw_s[at] = live
-
-    for i in (2, 3, 4, 5):
-        copies[i].wait()
-    pl.semaphore_wait(barrier, 2 + (n_gy - 1) + (n_gx - 1))
-
-    def halo(window, k):
-        return [
-            remote(window.at[pl.ds(8, 8)], window.at[pl.ds(0, 8)], halo_send.at[k, 0], halo_recv.at[k, 0], right),
-            remote(window.at[pl.ds(8, 8)], window.at[pl.ds(16, 8)], halo_send.at[k, 1], halo_recv.at[k, 1], left),
-        ]
-
-    halo0 = halo(xw0, 0)
-    for copy in halo0:
-        copy.start()
-    cf_halo = [
-        remote(cfw.at[1], cfw.at[0], cf_send.at[0], cf_recv.at[0], right),
-        remote(cfw.at[1], cfw.at[2], cf_send.at[1], cf_recv.at[1], left),
-    ]
-    for copy in cf_halo:
-        copy.start()
 
     iota_hi = lax.broadcasted_iota(jnp.int32, (WINDOW, LANES), 0)
     iota_lo = lax.broadcasted_iota(jnp.int32, (LANES, LANES), 0)
@@ -146,30 +152,17 @@
                 jnp.concatenate(left_parts, axis=1), jnp.concatenate(ones, axis=1), NT, preferred_element_type=F32
             )
 
-        total = lax.fori_loop(0, SUPPORT, step, jnp.zeros((WINDOW * count, LANES), F32))
+        total = lax.fori_loop(0, SUPPORT, step, jnp.zeros((WINDOW * count, LANES), F32), unroll=9)
         out = [total[:24] + total[24:48]]
         if with_abs:
             out.append(total[48:72] + total[72:96])
         return out
-
-    def send_spread(parts, out, into, k):
-        for i, part in enumerate(parts):
-            out[0, 8 * i : 8 * i + 8, :] = part[0:8]
-            out[1, 8 * i : 8 * i + 8, :] = part[16:24]
-        copies = [
-            remote(out.at[0], into.at[0], sp_send.at[k, 0], sp_recv.at[k, 0], left),
-            remote(out.at[1], into.at[1], sp_send.at[k, 1], sp_recv.at[k, 1], right),
-        ]
-        for copy in copies:
-            copy.start()
-        return copies
 
     def forward(window, with_abs):
         def row(r, carry):
             near_rows = [spread_rows(window[pl.ds(r + k, 1), :], (8, LANES)) for k in range(CLASSES)]
             lanes = pl.ds(pl.multiple_of(r * LANES, LANES), LANES)
             total = jnp.zeros((8, LANES), F32)
-            squares = jnp.zeros((8, LANES), F32)
             weight = jnp.zeros((8, LANES), F32)
             for b in range(4):
                 hi = hi_s[8 * b : 8 * b + 8, lanes]
@@ -180,87 +173,78 @@
                     got = jnp.where(hi == k, jnp.take_along_axis(near_rows[k], lo, axis=1, mode="promise_in_bounds"), got)
                 total = total + w * got
                 if with_abs:
-                    size = jnp.abs(w)
-                    squares = squares + size * (got * got)
-                    weight = weight + size
+                    weight = weight + jnp.abs(w)
             fwd[pl.ds(r, 1), :] = jnp.sum(total, axis=0, keepdims=True)
             if with_abs:
-                quad[pl.ds(r, 1), :] = jnp.sum(squares, axis=0, keepdims=True)
                 rabs[pl.ds(r, 1), :] = jnp.sum(weight, axis=0, keepdims=True)
             return carry
 
         lax.fori_loop(0, ROWS, row, 0)
 
-    def gather_first(k, tile):
-        ag[k, gy] = tile
+    def gather_first(tile):
+        ag[gy] = tile
         copies = []
         for d in range(1, n_gy):
-            copies.append(
-                remote(ag.at[k, gy], ag.at[k, gy], ag_send.at[k, d], ag_recv.at[k, d], (gx, lax.rem(gy + d, n_gy)))
-            )
+            copies.append(remote(ag.at[gy], ag.at[gy], ag_send.at[d], ag_recv.at[d], (gx, lax.rem(gy + d, n_gy))))
             copies[-1].start()
         return copies
 
-    def gather_second(k, copies):
-        for copy in copies:
-            copy.wait()
-        agx[k, gx] = jnp.sum(ag[k], axis=0)
+    def gather_second(copies):
+        arrive(copies)
+        agx[gx] = jnp.sum(ag[...], axis=0)
         copies = []
         for d in range(1, n_gx):
-            copies.append(
-                remote(agx.at[k, gx], agx.at[k, gx], agx_send.at[k, d], agx_recv.at[k, d], (lax.rem(gx + d, n_gx), gy))
-            )
+            copies.append(remote(agx.at[gx], agx.at[gx], agx_send.at[d], agx_recv.at[d], (lax.rem(gx + d, n_gx), gy)))
             copies[-1].start()
         return copies
 
-    def gather_end(k, copies):
-        for copy in copies:
-            copy.wait()
-        total = jnp.sum(jnp.sum(agx[k], axis=0), axis=1, keepdims=True)
-        return total[0:1], total[1:2]
-
-    def tile_of(first, second):
-        return jnp.concatenate(
-            [
-                jnp.sum(first, axis=0, keepdims=True),
-                jnp.sum(second, axis=0, keepdims=True),
-                jnp.zeros((6, LANES), F32),
-            ],
-            axis=0,
-        )
-
-    def split_off(parts, out, into, k, keep):
-        for i, part in enumerate(parts):
-            keep[8 * i : 8 * i + 8, :] = part[8:16]
-        return send_spread(parts, out, into, k)
-
-    spread0 = split_off(scatter(row0, True), sp_out0, sp_in0, 0, mid0)
-    for copy in halo0:
-        copy.wait()
+    def gather_end(copies):
+        arrive(copies)
+        total = jnp.sum(jnp.sum(agx[...], axis=0), axis=1, keepdims=True)
+        return [total[i : i + 1] for i in range(4)]
+
+    def tile_of(*fields):
+        rows = [jnp.sum(field, axis=0, keepdims=True) for field in fields]
+        return jnp.concatenate(rows + [jnp.zeros((8 - len(rows), LANES), F32)], axis=0)
+
+    back, size = scatter(row0, True)
+    arrive(halo0)
     forward(xw0, True)
     r0 = xw0[8:16, :]
-    first0 = gather_first(
-        0, tile_of(r0 * r0, (diag_v[...] + rabs[...]) * (r0 * r0) + quad[...] + 2.0 * r0 * fwd[...])
-    )
+    to_left[0:8, :] = back[0:8] + size[0:8] * xw0[0:8, :]
+    to_left[8:16, :] = size[0:8]
+    to_right[0:8, :] = back[16:24] + size[16:24] * xw0[16:24, :]
+    to_right[8:16, :] = size[16:24]
+    shift = diag_v[...] + rabs[...] + size[8:16]
+    part[...] = shift * r0 + fwd[...] + back[8:16]
+    shift_s[...] = shift
+    near_by = [
+        remote(part, from_left.at[pl.ds(0, 8)], ex_send.at[0], ex_recv.at[0], right),
+        remote(part, from_right.at[pl.ds(0, 8)], ex_send.at[1], ex_recv.at[1], left),
+        remote(to_right, from_left.at[pl.ds(8, 16)], ex_send.at[2], ex_recv.at[2], right),
+        remote(to_left, from_right.at[pl.ds(8, 16)], ex_send.at[3], ex_recv.at[3], left),
+        remote(to_right.at[pl.ds(0, 8)], from_left.at[pl.ds(24, 8)], ex_send.at[4], ex_recv.at[4], right2),
+        remote(to_left.at[pl.ds(0, 8)], from_right.at[pl.ds(24, 8)], ex_send.at[5], ex_recv.at[5], left2),
+    ]
+    for copy in near_by:
+        copy.start()
 
     for i in range(6, 12):
         copies[i].wait()
 
-    chunk = 512
+    chunk = 2048
 
     def mlp(i, carry):
         at = pl.ds(pl.multiple_of(i * chunk, chunk), chunk)
         hidden = lax.dot_general(w1_v[...], pin_v[:, at], TN, preferred_element_type=F32)
         hidden = jnp.maximum(hidden, 0.0).astype(BF16)
-        out = lax.dot_general(w2_v[...], hidden, TN, preferred_element_type=F32)
+        out = jnp.dot(w2_v[...], hidden, preferred_element_type=F32)
         feats[:, at] = out.astype(BF16).astype(F32)
         return carry
 
     lax.fori_loop(0, POINTS // chunk, mlp, 0)
-    second0 = gather_second(0, first0)
-
-    for copy in cf_halo:
-        copy.wait()
+
+    arrive(cf_halo)
     for side in range(3):
         fwin[:, COARSE * side : COARSE * (side + 1)] = cfw[side].astype(F32)
 
@@ -281,28 +265,29 @@
                 near[c, e, 8 * b : 8 * b + 8, :] = got
         return carry
 
-    lax.fori_loop(0, WIDTH, support_features, 0)
-
-    rr0, dad0 = gather_end(0, second0)
-    alpha0 = rr0 / dad0
-    for copy in spread0:
-        copy.wait()
-    shift_s[...] = diag_v[...] + rabs[...] + (mid0[8:16, :] + sp_in0[0, 8:16, :] + sp_in0[1, 8:16, :])
-    q0_s[...] = shift_s[...] * r0 + fwd[...] + (mid0[0:8, :] + sp_in0[0, 0:8, :] + sp_in0[1, 0:8, :])
-    r1 = r0 - alpha0 * q0_s[...]
-    xw1[8:16, :] = r1
-    halo1 = halo(xw1, 1)
-    for copy in halo1:
+    lax.fori_loop(0, WIDTH, support_features, 0, unroll=4)
+
+    arrive(near_by)
+    xw1[0:8, :] = from_left[0:8, :] + to_left[0:8, :] + from_left[24:32, :]
+    xw1[8:16, :] = part[...] + from_left[8:16, :] + from_right[8:16, :]
+    xw1[16:24, :] = from_right[0:8, :] + to_right[0:8, :] + from_right[24:32, :]
+    shift_s[...] = shift_s[...] + (from_left[16:24, :] + from_right[16:24, :])
+    forward(xw1, False)
+    q0 = xw1[8:16, :]
+    first = gather_first(tile_of(r0 * r0, r0 * q0, q0 * q0, shift_s[...] * (q0 * q0) + 2.0 * q0 * fwd[...]))
+    for r in range(ROWS):
+        row1[0:1, LANES * r : LANES * (r + 1)] = q0[r : r + 1]
+
+    (back,) = scatter(row1, False)
+    to_left1[...] = back[0:8]
+    to_right1[...] = back[16:24]
+    mid1[...] = back[8:16]
+    ends = [
+        remote(to_right1, from_left1, ex_send.at[6], ex_recv.at[6], right),
+        remote(to_left1, from_right1, ex_send.at[7], ex_recv.at[7], left),
+    ]
+    for copy in ends:
         copy.start()
-    for r in range(ROWS):
-        row1[0:1, LANES * r : LANES * (r + 1)] = r1[r : r + 1]
-
-    spread1 = split_off(scatter(row1, False), sp_out1, sp_in1, 1, mid1)
-    for copy in halo1:
-        copy.wait()
-    forward(xw1, False)
-    r1 = xw1[8:16, :]
-    first1 = gather_first(1, tile_of(r1 * r1, shift_s[...] * (r1 * r1) + 2.0 * r1 * fwd[...]))
 
     iota_j = lax.broadcasted_iota(jnp.int32, (32, LANES), 0)
     digit = [lax.div(iota_j, 9), lax.rem(lax.div(iota_j, 3), 3), lax.rem(iota_j, 3)]
@@ -335,7 +320,7 @@
         return carry
 
     lax.fori_loop(0, 2 * SLOTS // group, kernel_values, 0)
-    second1 = gather_second(1, first1)
+    second = gather_second(first)
 
     def gram_rows(i, carry):
         c = lax.rem(i, 2)
@@ -356,18 +341,25 @@
     out2 = pltpu.make_async_copy(gram_v, gram_o, out_sem.at[2])
     out2.start()
 
-    rr1, rar1 = gather_end(1, second1)
+    rr0, rq, qq, qaq = gather_end(second)
+    alpha0 = rr0 / rq
+    shear = rq / rr0
+    hh = qq - shear * rq
+    hah = qaq - 2.0 * shear * qq + shear * shear * rq
+    rr1 = alpha0 * alpha0 * hh
     beta = rr1 / rr0
-    alpha1 = rr1 / (rar1 - beta * rr1 / alpha0)
-    for copy in spread1:
-        copy.wait()
-    image = shift_s[...] * r1 + fwd[...] + (mid1[...] + sp_in1[0] + sp_in1[1])
+    alpha1 = rr1 / (alpha0 * alpha0 * hah - beta * rr1 * shear)
+    arrive(ends)
+    r1 = r0 - alpha0 * q0
+    image = shift_s[...] * q0 + fwd[...] + (mid1[...] + from_left1[...] + from_right1[...])
     sol_v[...] = alpha0 * r0 + alpha1 * (r1 + beta * r0)
-    res_v[...] = r1 - alpha1 * (image + beta * q0_s[...])
+    res_v[...] = r1 - alpha1 * ((1.0 + beta) * q0 - alpha0 * image)
     out0 = pltpu.make_async_copy(sol_v, sol_o, out_sem.at[0])
     out1 = pltpu.make_async_copy(res_v, res_o, out_sem.at[1])
     out0.start()
     out1.start()
+    for copy in started:
+        copy.wait_send()
     out0.wait()
     out1.wait()
     out2.wait()
@@ -396,7 +388,7 @@
             vm((2, LANES), jnp.int32),
             vm((SUPPORT, COARSE), jnp.int32),
             vm((WIDTH, HIDDEN), BF16),
-            vm((HIDDEN, WIDTH), BF16),
+            vm((WIDTH, HIDDEN), BF16),
             vm((32, 1024), jnp.int32),
             vm((32, 1024), jnp.int32),
             vm((32, 1024), F32),
@@ -411,13 +403,15 @@
             vm(fine, F32),
             vm(fine, F32),
             vm((16, LANES), F32),
-            vm((8, LANES), F32),
-            vm((2, 16, LANES), F32),
-            vm((2, 16, LANES), F32),
-            vm((2, 8, LANES), F32),
-            vm((2, 8, LANES), F32),
-            vm((2, n_gy, 8, LANES), F32),
-            vm((2, n_gx, 8, LANES), F32),
+            vm((16, LANES), F32),
+            vm((32, LANES), F32),
+            vm((32, LANES), F32),
+            vm(fine, F32),
+            vm(fine, F32),
+            vm(fine, F32),
+            vm(fine, F32),
+            vm((n_gy, 8, LANES), F32),
+            vm((n_gx, 8, LANES), F32),
             vm((3, WIDTH, COARSE), BF16),
             vm((WIDTH, 3 * COARSE), F32),
             vm((WIDTH, POINTS), F32),
@@ -425,24 +419,24 @@
             vm((2, SLOTS, 32, LANES), F32),
             vm((SUPPORT, SUPPORT, COARSE), BF16),
             dma((12,)),
-            dma((2, 2)),
-            dma((2, 2)),
             dma((2,)),
             dma((2,)),
-            dma((2, 2)),
-            dma((2, 2)),
-            dma((2, n_gy)),
-            dma((2, n_gy)),
-            dma((2, n_gx)),
-            dma((2, n_gx)),
+            dma((2,)),
+            dma((2,)),
+            dma((8,)),
+            dma((8,)),
+            dma((n_gy,)),
+            dma((n_gy,)),
+            dma((n_gx,)),
+            dma((n_gx,)),
             dma((3,)),
         ],
         compiler_params=pltpu.CompilerParams(
-            collective_id=0, has_side_effects=True, vmem_limit_bytes=48 * 1024 * 1024
+            collective_id=0, has_side_effects=True, vmem_limit_bytes=62 * 1024 * 1024
         ),
     )(
         rhs.reshape(fine), rhs.reshape(1, 1024), diag.reshape(fine), sup, wts, pin, off,
-        cnt.reshape(2, LANES), cf, cs, w1, w2,
+        cnt.reshape(2, LANES), cf, cs, w1, w2.T,
     )
     return sol.reshape(1024), res.reshape(1024), gram
 

time: 53.4 us -> 35 us (0.66)
  Pallas kernels: 44.5 us -> 30.4 us
  local copies, waits for them, and re-layouts: 7.81 us -> 3.74 us
    pallas_call x1, Pallas kernels: 44.5 us -> 30.4 us  [on_device(): pl.pallas_call(functools.partial(kernel, n_gx, n_gy), out_shape=[jax.Shap...]
    unnamed x24 -> x7, local copies, waits for them, and re-layouts: 7.81 us -> 3.74 us
where the time goes in v2:
time: 35 us; the launch traced here: 34.8 us
  Pallas kernels  30.4 us (87%)
  local copies, waits for them, and re-layouts  3.74 us (11%)
  between operations  0.65 us (2%)
    pallas_call x1, Pallas kernels, on_device(): pl.pallas_call(functools.partial(kernel, n_gx, n_gy), out_shape=[jax.Shap...  30.4 us
    unnamed x7, local copies, waits for them, and re-layouts  3.74 us

profile of v2, /device:TPU:1, one launch (start us, length us, event | category | flops | bytes accessed | tf_op | source)
XLA Modules:
  0.0 34.8 jit_solution(11690347892772632780)
XLA Ops:
  0.6 30.4 %shard_map.130 = (f32[8,128]{1,0:T(8,128)}, f32[8,128]{1,0:T(8,128)}, bf16[27,27,256]{2,1,0:T(8,128)(2,1)}) custom-call(f32[8,128]{1,0:T(8,128)} %bitcast.7, f32[1,1024]{1,0:T(1,128)} %bitcast.8, f32[8,128]{1,0:T(8,128)} %bitcast.10, s32[27,1024]{1,0:T(8,128)} %sup.1, f32[27,1024]{1,0:T(8,128)} %wts.1, bf16[32,4096]{1,0:T(8,128)(2,1)} %pin.1, ...), custom_call_target="tpu_custom_call" | custom-call | tf_op jit(solution)/shard_map/pallas_call | solution.py:372
  31.0 0.0 copy-start.1
  31.0 0.7 %copy-done.1 = f32[8,128]{1,0:T(8,128)S(1)} copy-done((f32[8,128]{1,0:T(8,128)S(1)}, f32[8,128]{1,0:T(8,128)}, u32[]{:S(2)}) %copy-start.1) | copy-done | bytes 4120
  31.7 0.0 copy-start
  31.7 0.6 %copy.17 = f32[1024]{0:T(1024)} copy(f32[1024]{0:T(1024)S(1)} %bitcast.12) | data formatting | bytes 8192
  32.3 0.1 copy-done
  32.4 0.6 %copy.18 = f32[1024]{0:T(1024)} copy(f32[1024]{0:T(1024)S(1)} %bitcast.11) | data formatting | bytes 8192
  33.0 1.8 %copy.19 = bf16[27,27,256]{2,1,0:T(8,128)(2,1)} copy(bf16[27,27,256]{2,1,0:T(8,128)(2,1)} %get-tuple-element.14) | data formatting | bytes 746496
Async XLA Ops:
  31.0 0.7 %copy-start.1 = (f32[8,128]{1,0:T(8,128)S(1)}, f32[8,128]{1,0:T(8,128)}, u32[]{:S(2)}) copy-start(f32[8,128]{1,0:T(8,128)} %get-tuple-element.6) | copy-start | bytes 12292
  31.7 0.7 %copy-start = (f32[8,128]{1,0:T(8,128)S(1)}, f32[8,128]{1,0:T(8,128)}, u32[]{:S(2)}) copy-start(f32[8,128]{1,0:T(8,128)} %get-tuple-element.7) | copy-start | bytes 12292

commit v3 on v2

--- a/solution.py
+++ b/solution.py
@@ -34,12 +34,12 @@
     rhs, rhs_row, diag, sup, wts, pin, off, cnt, cf, cs, w1, w2,
     sol_o, res_o, gram_o,
     row0, diag_v, sup_v, wts_v, pin_v, off_v, cnt_v, cs_v, w1_v, w2_v,
-    hi_s, lo_s, lw_s, xw0, xw1, row1, fwd, rabs, shift_s, part, mid1, sol_v, res_v,
+    hi_s, lo_s, lw_s, xw0, xw1, row1, fwd, rabs, shift_s, part, mid1,
     to_left, to_right, from_left, from_right, to_left1, to_right1, from_left1, from_right1,
     ag, agx,
-    cfw, fwin, feats, near, kern, gram_v,
+    cfw, table, feats, near, kern,
     in_sem, halo_send, halo_recv, cf_send, cf_recv, ex_send, ex_recv,
-    ag_send, ag_recv, agx_send, agx_recv, out_sem,
+    ag_send, ag_recv, agx_send, agx_recv,
 ):
     gx = lax.axis_index("gx")
     gy = lax.axis_index("gy")
@@ -51,6 +51,9 @@
         return lax.div(other, n_gy), lax.rem(other, n_gy)
 
     left2, left, right, right2 = device(-2), device(-1), device(1), device(2)
+
+    plane = [(gx, lax.rem(gy + d, n_gy)) for d in range(1, n_gy)]
+    column = [(lax.rem(gx + d, n_gx), gy) for d in range(1, n_gx)]
 
     moves = [
         (rhs, xw0.at[pl.ds(8, 8)]), (cf, cfw.at[1]), (sup, sup_v), (wts, wts_v), (rhs_row, row0), (diag, diag_v),
@@ -61,12 +64,8 @@
         copy.start()
 
     barrier = pltpu.get_barrier_semaphore()
-    for other in (left, right, left2, right2):
+    for other in (left, right, left2, right2, *plane, *column):
         pl.semaphore_signal(barrier, inc=1, device_id=other, device_id_type=MESH)
-    for d in range(1, n_gy):
-        pl.semaphore_signal(barrier, inc=1, device_id=(gx, lax.rem(gy + d, n_gy)), device_id_type=MESH)
-    for d in range(1, n_gx):
-        pl.semaphore_signal(barrier, inc=1, device_id=(lax.rem(gx + d, n_gx), gy), device_id_type=MESH)
 
     def remote(src, dst, send, recv, device):
         return pltpu.make_async_remote_copy(
@@ -75,7 +74,7 @@
 
     for i in (0, 1):
         copies[i].wait()
-    pl.semaphore_wait(barrier, 4 + (n_gy - 1) + (n_gx - 1))
+    pl.semaphore_wait(barrier, 4 + len(plane) + len(column))
 
     started = []
 
@@ -179,35 +178,48 @@
                 rabs[pl.ds(r, 1), :] = jnp.sum(weight, axis=0, keepdims=True)
             return carry
 
-        lax.fori_loop(0, ROWS, row, 0)
-
-    def gather_first(tile):
-        ag[gy] = tile
-        copies = []
-        for d in range(1, n_gy):
-            copies.append(remote(ag.at[gy], ag.at[gy], ag_send.at[d], ag_recv.at[d], (gx, lax.rem(gy + d, n_gy))))
-            copies[-1].start()
+        lax.fori_loop(0, ROWS, row, 0, unroll=4)
+
+    lane_group = lax.div(lax.broadcasted_iota(jnp.int32, (1, LANES), 1), 32)
+
+    def row_of(*fields):
+        row = jnp.zeros((1, LANES), F32)
+        for i, field in enumerate(fields):
+            part = jnp.sum(field, axis=0, keepdims=True)
+            part = part + pltpu.roll(part, 64, 1)
+            part = part + pltpu.roll(part, 32, 1)
+            row = jnp.where(lane_group == i, part, row)
+        return row
+
+    def to_others(slots, me, row, send, recv, others):
+        slots[me] = row
+        copies = [
+            remote(slots.at[me], slots.at[me], send.at[i], recv.at[i], other) for i, other in enumerate(others)
+        ]
+        for copy in copies:
+            copy.start()
         return copies
 
-    def gather_second(copies):
+    def sum_of(slots, copies):
         arrive(copies)
-        agx[gx] = jnp.sum(ag[...], axis=0)
-        copies = []
-        for d in range(1, n_gx):
-            copies.append(remote(agx.at[gx], agx.at[gx], agx_send.at[d], agx_recv.at[d], (lax.rem(gx + d, n_gx), gy)))
-            copies[-1].start()
-        return copies
-
-    def gather_end(copies):
-        arrive(copies)
-        total = jnp.sum(jnp.sum(agx[...], axis=0), axis=1, keepdims=True)
-        return [total[i : i + 1] for i in range(4)]
-
-    def tile_of(*fields):
-        rows = [jnp.sum(field, axis=0, keepdims=True) for field in fields]
-        return jnp.concatenate(rows + [jnp.zeros((8 - len(rows), LANES), F32)], axis=0)
+        return jnp.sum(slots[...], axis=0)
 
     back, size = scatter(row0, True)
+    for i in range(6, 12):
+        copies[i].wait()
+
+    chunk = 2048
+
+    def mlp(i, carry):
+        at = pl.ds(pl.multiple_of(i * chunk, chunk), chunk)
+        hidden = lax.dot_general(w1_v[...], pin_v[:, at], TN, preferred_element_type=F32)
+        hidden = jnp.maximum(hidden, 0.0).astype(BF16)
+        out = jnp.dot(w2_v[...], hidden, preferred_element_type=F32)
+        feats[:, at] = out.astype(BF16).astype(F32)
+        return carry
+
+    lax.fori_loop(0, POINTS // chunk, mlp, 0)
+
     arrive(halo0)
     forward(xw0, True)
     r0 = xw0[8:16, :]
@@ -229,68 +241,33 @@
     for copy in near_by:
         copy.start()
 
-    for i in range(6, 12):
-        copies[i].wait()
-
-    chunk = 2048
-
-    def mlp(i, carry):
-        at = pl.ds(pl.multiple_of(i * chunk, chunk), chunk)
-        hidden = lax.dot_general(w1_v[...], pin_v[:, at], TN, preferred_element_type=F32)
-        hidden = jnp.maximum(hidden, 0.0).astype(BF16)
-        out = jnp.dot(w2_v[...], hidden, preferred_element_type=F32)
-        feats[:, at] = out.astype(BF16).astype(F32)
+    arrive(cf_halo)
+    for k in range(6):
+        table[WIDTH * k : WIDTH * (k + 1), :] = cfw[k // 2][:, LANES * (k % 2) : LANES * (k % 2 + 1)]
+    iota_far = lax.broadcasted_iota(jnp.int32, (LANES, COARSE), 0)
+
+    def support_features(j, carry):
+        value = cs_v[pl.ds(j, 1), :]
+        hi = spread_rows(lax.shift_right_arithmetic(value, 7), (8, COARSE))
+        lo = spread_rows(jnp.bitwise_and(value, 127), (LANES, COARSE))
+        ones = jnp.where(lo == iota_far, 1.0, 0.0).astype(BF16)
+        got = jnp.dot(table[...], ones, preferred_element_type=F32)
+        hits = [hi == k for k in range(6)]
+        for q in range(4):
+            picked = jnp.zeros((8, COARSE), F32)
+            for k in range(6):
+                picked = jnp.where(hits[k], got[WIDTH * k + 8 * q : WIDTH * k + 8 * q + 8], picked)
+            for c in range(2):
+                near[c, pl.ds(32 * 8 * q + j, 8, stride=32), :] = picked[:, LANES * c : LANES * (c + 1)]
         return carry
 
-    lax.fori_loop(0, POINTS // chunk, mlp, 0)
-
-    arrive(cf_halo)
-    for side in range(3):
-        fwin[:, COARSE * side : COARSE * (side + 1)] = cfw[side].astype(F32)
-
-    def support_features(e, carry):
-        line = fwin[pl.ds(e, 1), :]
-        sources = [spread_rows(line[:, LANES * k : LANES * (k + 1)], (8, LANES)) for k in range(6)]
-        for c in range(2):
-            for b in range(4):
-                rows = 8 if b < 3 else 3
-                value = cs_v[8 * b : 8 * b + rows, LANES * c : LANES * (c + 1)]
-                if rows < 8:
-                    value = jnp.concatenate([value, jnp.full((8 - rows, LANES), -1, jnp.int32)], axis=0)
-                hi = lax.shift_right_arithmetic(value, 7)
-                lo = jnp.bitwise_and(value, 127)
-                got = jnp.zeros((8, LANES), F32)
-                for k in range(6):
-                    got = jnp.where(hi == k, jnp.take_along_axis(sources[k], lo, axis=1, mode="promise_in_bounds"), got)
-                near[c, e, 8 * b : 8 * b + 8, :] = got
-        return carry
-
-    lax.fori_loop(0, WIDTH, support_features, 0, unroll=4)
-
-    arrive(near_by)
-    xw1[0:8, :] = from_left[0:8, :] + to_left[0:8, :] + from_left[24:32, :]
-    xw1[8:16, :] = part[...] + from_left[8:16, :] + from_right[8:16, :]
-    xw1[16:24, :] = from_right[0:8, :] + to_right[0:8, :] + from_right[24:32, :]
-    shift_s[...] = shift_s[...] + (from_left[16:24, :] + from_right[16:24, :])
-    forward(xw1, False)
-    q0 = xw1[8:16, :]
-    first = gather_first(tile_of(r0 * r0, r0 * q0, q0 * q0, shift_s[...] * (q0 * q0) + 2.0 * q0 * fwd[...]))
-    for r in range(ROWS):
-        row1[0:1, LANES * r : LANES * (r + 1)] = q0[r : r + 1]
-
-    (back,) = scatter(row1, False)
-    to_left1[...] = back[0:8]
-    to_right1[...] = back[16:24]
-    mid1[...] = back[8:16]
-    ends = [
-        remote(to_right1, from_left1, ex_send.at[6], ex_recv.at[6], right),
-        remote(to_left1, from_right1, ex_send.at[7], ex_recv.at[7], left),
-    ]
-    for copy in ends:
-        copy.start()
+    lax.fori_loop(0, SUPPORT, support_features, 0, unroll=3)
 
     iota_j = lax.broadcasted_iota(jnp.int32, (32, LANES), 0)
-    digit = [lax.div(iota_j, 9), lax.rem(lax.div(iota_j, 3), 3), lax.rem(iota_j, 3)]
+    tops = jnp.where(iota_j >= 18, 2, jnp.where(iota_j >= 9, 1, 0))
+    rest = iota_j - 9 * tops
+    middles = jnp.where(rest >= 6, 2, jnp.where(rest >= 3, 1, 0))
+    digit = [tops, middles, rest - 3 * middles]
     group = 4
 
     def kernel_values(i, carry):
@@ -299,7 +276,7 @@
         points = [pl.ds(pl.multiple_of((s0 + g) * COARSE + c * LANES, LANES), LANES) for g in range(group)]
         dots = [[jnp.zeros((8, LANES), F32) for _ in range(4)] for _ in range(group)]
         for e in range(WIDTH):
-            sources = [near[c, e, 8 * b : 8 * b + 8, :] for b in range(4)]
+            sources = [near[c, pl.ds(32 * e + 8 * b, 8), :] for b in range(4)]
             for g in range(group):
                 feat = spread_rows(feats[e : e + 1, points[g]], (8, LANES))
                 dots[g] = [dots[g][b] + feat * sources[b] for b in range(4)]
@@ -320,7 +297,30 @@
         return carry
 
     lax.fori_loop(0, 2 * SLOTS // group, kernel_values, 0)
-    second = gather_second(first)
+
+    arrive(near_by)
+    xw1[0:8, :] = from_left[0:8, :] + to_left[0:8, :] + from_left[24:32, :]
+    xw1[8:16, :] = part[...] + from_left[8:16, :] + from_right[8:16, :]
+    xw1[16:24, :] = from_right[0:8, :] + to_right[0:8, :] + from_right[24:32, :]
+    shift_s[...] = shift_s[...] + (from_left[16:24, :] + from_right[16:24, :])
+    forward(xw1, False)
+    q0 = xw1[8:16, :]
+    first = to_others(ag, gy, row_of(r0 * r0, r0 * q0, q0 * q0, shift_s[...] * (q0 * q0) + 2.0 * q0 * fwd[...]), ag_send, ag_recv, plane)
+    for r in range(ROWS):
+        row1[0:1, LANES * r : LANES * (r + 1)] = q0[r : r + 1]
+
+    (back,) = scatter(row1, False)
+    to_left1[...] = back[0:8]
+    to_right1[...] = back[16:24]
+    mid1[...] = back[8:16]
+    ends = [
+        remote(to_right1, from_left1, ex_send.at[6], ex_recv.at[6], right),
+        remote(to_left1, from_right1, ex_send.at[7], ex_recv.at[7], left),
+    ]
+    for copy in ends:
+        copy.start()
+
+    second = to_others(agx, gx, sum_of(ag, first), agx_send, agx_recv, column)
 
     def gram_rows(i, carry):
         c = lax.rem(i, 2)
@@ -334,14 +334,12 @@
                 sums[g] = [sums[g][b] + one * columns[b] for b in range(4)]
         for g in range(3):
             whole = jnp.concatenate(sums[g], axis=0).astype(BF16)
-            gram_v[j0 + g, :, here] = whole[:SUPPORT]
+            gram_o[j0 + g, :, here] = whole[:SUPPORT]
         return carry
 
     lax.fori_loop(0, 18, gram_rows, 0)
-    out2 = pltpu.make_async_copy(gram_v, gram_o, out_sem.at[2])
-    out2.start()
-
-    rr0, rq, qq, qaq = gather_end(second)
+    row = sum_of(agx, second)
+    rr0, rq, qq, qaq = [jnp.sum(jnp.where(lane_group == i, row, 0.0), axis=1, keepdims=True) for i in range(4)]
     alpha0 = rr0 / rq
     shear = rq / rr0
     hh = qq - shear * rq
@@ -352,17 +350,19 @@
     arrive(ends)
     r1 = r0 - alpha0 * q0
     image = shift_s[...] * q0 + fwd[...] + (mid1[...] + from_left1[...] + from_right1[...])
-    sol_v[...] = alpha0 * r0 + alpha1 * (r1 + beta * r0)
-    res_v[...] = r1 - alpha1 * ((1.0 + beta) * q0 - alpha0 * image)
-    out0 = pltpu.make_async_copy(sol_v, sol_o, out_sem.at[0])
-    out1 = pltpu.make_async_copy(res_v, res_o, out_sem.at[1])
-    out0.start()
-    out1.start()
+    sol_o[...] = alpha0 * r0 + alpha1 * (r1 + beta * r0)
+    res_o[...] = r1 - alpha1 * ((1.0 + beta) * q0 - alpha0 * image)
     for copy in started:
         copy.wait_send()
-    out0.wait()
-    out1.wait()
-    out2.wait()
+
+
+def hand_over(sol, res, gram, sol_o, res_o, gram_o, sem):
+    pairs = [(gram, gram_o), (sol, sol_o), (res, res_o)]
+    copies = [pltpu.make_async_copy(src, dst, sem.at[i]) for i, (src, dst) in enumerate(pairs)]
+    for copy in copies:
+        copy.start()
+    for copy in copies:
+        copy.wait()
 
 
 def on_device(n_gx, n_gy, rhs, diag, sup, wts, pin, off, cnt, cf, cs, w1, w2):
@@ -372,12 +372,12 @@
     sol, res, gram = pl.pallas_call(
         functools.partial(kernel, n_gx, n_gy),
         out_shape=[
-            jax.ShapeDtypeStruct(fine, F32),
-            jax.ShapeDtypeStruct(fine, F32),
-            jax.ShapeDtypeStruct((SUPPORT, SUPPORT, COARSE), BF16),
+            pltpu.VMEM(fine, F32),
+            pltpu.VMEM(fine, F32),
+            pltpu.VMEM((SUPPORT, SUPPORT, COARSE), BF16),
         ],
         in_specs=[pl.BlockSpec(memory_space=pl.ANY)] * 12,
-        out_specs=[pl.BlockSpec(memory_space=pl.ANY)] * 3,
+        out_specs=[pl.BlockSpec(memory_space=pltpu.VMEM)] * 3,
         scratch_shapes=[
             vm((1, 1024), F32),
             vm(fine, F32),
@@ -400,8 +400,6 @@
             vm(fine, F32),
             vm(fine, F32),
             vm(fine, F32),
-            vm(fine, F32),
-            vm(fine, F32),
             vm((16, LANES), F32),
             vm((16, LANES), F32),
             vm((32, LANES), F32),
@@ -410,14 +408,13 @@
             vm(fine, F32),
             vm(fine, F32),
             vm(fine, F32),
-            vm((n_gy, 8, LANES), F32),
-            vm((n_gx, 8, LANES), F32),
+            vm((n_gy, 1, LANES), F32),
+            vm((n_gx, 1, LANES), F32),
             vm((3, WIDTH, COARSE), BF16),
-            vm((WIDTH, 3 * COARSE), F32),
+            vm((6 * WIDTH, LANES), BF16),
             vm((WIDTH, POINTS), F32),
-            vm((2, WIDTH, 32, LANES), F32),
+            vm((2, WIDTH * 32, LANES), F32),
             vm((2, SLOTS, 32, LANES), F32),
-            vm((SUPPORT, SUPPORT, COARSE), BF16),
             dma((12,)),
             dma((2,)),
             dma((2,)),
@@ -425,11 +422,10 @@
             dma((2,)),
             dma((8,)),
             dma((8,)),
-            dma((n_gy,)),
-            dma((n_gy,)),
-            dma((n_gx,)),
-            dma((n_gx,)),
-            dma((3,)),
+            dma((n_gy - 1,)),
+            dma((n_gy - 1,)),
+            dma((n_gx - 1,)),
+            dma((n_gx - 1,)),
         ],
         compiler_params=pltpu.CompilerParams(
             collective_id=0, has_side_effects=True, vmem_limit_bytes=62 * 1024 * 1024
@@ -438,6 +434,18 @@
         rhs.reshape(fine), rhs.reshape(1, 1024), diag.reshape(fine), sup, wts, pin, off,
         cnt.reshape(2, LANES), cf, cs, w1, w2.T,
     )
+    sol, res, gram = pl.pallas_call(
+        hand_over,
+        out_shape=[
+            jax.ShapeDtypeStruct(fine, F32),
+            jax.ShapeDtypeStruct(fine, F32),
+            jax.ShapeDtypeStruct((SUPPORT, SUPPORT, COARSE), BF16),
+        ],
+        in_specs=[pl.BlockSpec(memory_space=pl.ANY)] * 3,
+        out_specs=[pl.BlockSpec(memory_space=pl.ANY)] * 3,
+        scratch_shapes=[dma((3,))],
+        compiler_params=pltpu.CompilerParams(vmem_limit_bytes=4 * 1024 * 1024),
+    )(sol, res, gram)
     return sol.reshape(1024), res.reshape(1024), gram
 
 

time: 35 us -> 29.5 us (0.84)
  local copies, waits for them, and re-layouts: 3.74 us -> 0 us
  Pallas kernels: 30.4 us -> 28.4 us
    unnamed x7 -> x0, local copies, waits for them, and re-layouts: 3.74 us -> none
    pallas_call x1 -> x2, Pallas kernels: 30.4 us -> 28.4 us  [the longest x1 27.6 us: on_device(): pl.pallas_call(functools.partial(kernel, n_gx, n_gy), out_shape=[pltpu.VM...]
where the time goes in v3:
time: 29.5 us; the launch traced here: 29 us
  Pallas kernels  28.4 us (96%)
  between operations  0.64 us (2%)
    pallas_call x1, Pallas kernels, on_device(): pl.pallas_call(functools.partial(kernel, n_gx, n_gy), out_shape=[pltpu.VM...  27.6 us
    pallas_call x1, Pallas kernels, on_device(): pl.pallas_call(hand_over, out_shape=[jax.ShapeDtypeStruct(fine, F32), jax...  0.79 us

profile of v3, /device:TPU:1, one launch (start us, length us, event | category | flops | bytes accessed | tf_op | source)
XLA Modules:
  0.0 29.0 jit_solution(16046697236940590850)
XLA Ops:
  0.6 27.6 %shard_map.130 = (f32[8,128]{1,0:T(8,128)S(1)}, f32[8,128]{1,0:T(8,128)S(1)}, bf16[27,27,256]{2,1,0:T(8,128)(2,1)S(1)}) custom-call(f32[8,128]{1,0:T(8,128)} %bitcast.7, f32[1,1024]{1,0:T(1,128)} %bitcast.8, f32[8,128]{1,0:T(8,128)} %bitcast.10, s32[27,1024]{1,0:T(8,128)} %sup.1, f32[27,1024]{1,0:T(8,128)} %wts.1, bf16[32,4096]{1,0:T(8,128)(2,1)} %pin.1, ...), custom_call_target="tpu_custom_call" | custom-call | tf_op jit(solution)/shard_map/pallas_call | solution.py:372
  28.2 0.8 %shard_map.131 = (f32[8,128]{1,0:T(8,128)}, f32[8,128]{1,0:T(8,128)}, bf16[27,27,256]{2,1,0:T(8,128)(2,1)}) custom-call(f32[8,128]{1,0:T(8,128)S(1)} %get-tuple-element.9.sol, f32[8,128]{1,0:T(8,128)S(1)} %get-tuple-element.10.res, bf16[27,27,256]{2,1,0:T(8,128)(2,1)S(1)} %get-tuple-element.11.gram), custom_call_target="tpu_custom_call" | custom-call | tf_op jit(solution)/shard_map/pallas_call | solution.py:437

commit v4 on v3

--- a/solution.py
+++ b/solution.py
@@ -37,7 +37,7 @@
     hi_s, lo_s, lw_s, xw0, xw1, row1, fwd, rabs, shift_s, part, mid1,
     to_left, to_right, from_left, from_right, to_left1, to_right1, from_left1, from_right1,
     ag, agx,
-    cfw, table, feats, near, kern,
+    cfw, feats, near, kern,
     in_sem, halo_send, halo_recv, cf_send, cf_recv, ex_send, ex_recv,
     ag_send, ag_recv, agx_send, agx_recv,
 ):
@@ -60,41 +60,18 @@
         (pin, pin_v), (w1, w1_v), (w2, w2_v), (cs, cs_v), (off, off_v), (cnt, cnt_v),
     ]
     copies = [pltpu.make_async_copy(src, dst, in_sem.at[i]) for i, (src, dst) in enumerate(moves)]
-    for copy in copies:
-        copy.start()
+    copies[0].start()
 
     barrier = pltpu.get_barrier_semaphore()
     for other in (left, right, left2, right2, *plane, *column):
         pl.semaphore_signal(barrier, inc=1, device_id=other, device_id_type=MESH)
+    for copy in copies[1:]:
+        copy.start()
 
     def remote(src, dst, send, recv, device):
         return pltpu.make_async_remote_copy(
             src_ref=src, dst_ref=dst, send_sem=send, recv_sem=recv, device_id=device, device_id_type=MESH
         )
-
-    for i in (0, 1):
-        copies[i].wait()
-    pl.semaphore_wait(barrier, 4 + len(plane) + len(column))
-
-    started = []
-
-    def arrive(copies):
-        for copy in copies:
-            copy.wait_recv()
-        started.extend(copies)
-
-    halo0 = [
-        remote(xw0.at[pl.ds(8, 8)], xw0.at[pl.ds(0, 8)], halo_send.at[0], halo_recv.at[0], right),
-        remote(xw0.at[pl.ds(8, 8)], xw0.at[pl.ds(16, 8)], halo_send.at[1], halo_recv.at[1], left),
-    ]
-    for copy in halo0:
-        copy.start()
-    cf_halo = [
-        remote(cfw.at[1], cfw.at[0], cf_send.at[0], cf_recv.at[0], right),
-        remote(cfw.at[1], cfw.at[2], cf_send.at[1], cf_recv.at[1], left),
-    ]
-    for copy in cf_halo:
-        copy.start()
 
     for i in range(2, 6):
         copies[i].wait()
@@ -117,6 +94,30 @@
             hi_s[at] = hi
             lo_s[at] = lo
             lw_s[at] = live
+
+    for i in (0, 1):
+        copies[i].wait()
+    pl.semaphore_wait(barrier, 4 + len(plane) + len(column))
+
+    started = []
+
+    def arrive(copies):
+        for copy in copies:
+            copy.wait_recv()
+        started.extend(copies)
+
+    halo0 = [
+        remote(xw0.at[pl.ds(8, 8)], xw0.at[pl.ds(0, 8)], halo_send.at[0], halo_recv.at[0], right),
+        remote(xw0.at[pl.ds(8, 8)], xw0.at[pl.ds(16, 8)], halo_send.at[1], halo_recv.at[1], left),
+    ]
+    for copy in halo0:
+        copy.start()
+    cf_halo = [
+        remote(cfw.at[1], cfw.at[0], cf_send.at[0], cf_recv.at[0], right),
+        remote(cfw.at[1], cfw.at[2], cf_send.at[1], cf_recv.at[1], left),
+    ]
+    for copy in cf_halo:
+        copy.start()
 
     iota_hi = lax.broadcasted_iota(jnp.int32, (WINDOW, LANES), 0)
     iota_lo = lax.broadcasted_iota(jnp.int32, (LANES, LANES), 0)
@@ -180,16 +181,8 @@
 
         lax.fori_loop(0, ROWS, row, 0, unroll=4)
 
-    lane_group = lax.div(lax.broadcasted_iota(jnp.int32, (1, LANES), 1), 32)
-
-    def row_of(*fields):
-        row = jnp.zeros((1, LANES), F32)
-        for i, field in enumerate(fields):
-            part = jnp.sum(field, axis=0, keepdims=True)
-            part = part + pltpu.roll(part, 64, 1)
-            part = part + pltpu.roll(part, 32, 1)
-            row = jnp.where(lane_group == i, part, row)
-        return row
+    def tile_of(*fields):
+        return jnp.concatenate([jnp.sum(field, axis=0, keepdims=True) for field in fields], axis=0)
 
     def to_others(slots, me, row, send, recv, others):
         slots[me] = row
@@ -242,20 +235,18 @@
         copy.start()
 
     arrive(cf_halo)
-    for k in range(6):
-        table[WIDTH * k : WIDTH * (k + 1), :] = cfw[k // 2][:, LANES * (k % 2) : LANES * (k % 2 + 1)]
-    iota_far = lax.broadcasted_iota(jnp.int32, (LANES, COARSE), 0)
+    iota_far = lax.broadcasted_iota(jnp.int32, (COARSE, COARSE), 0)
 
     def support_features(j, carry):
         value = cs_v[pl.ds(j, 1), :]
-        hi = spread_rows(lax.shift_right_arithmetic(value, 7), (8, COARSE))
-        lo = spread_rows(jnp.bitwise_and(value, 127), (LANES, COARSE))
-        ones = jnp.where(lo == iota_far, 1.0, 0.0).astype(BF16)
-        got = jnp.dot(table[...], ones, preferred_element_type=F32)
-        hits = [hi == k for k in range(6)]
+        side = spread_rows(lax.shift_right_arithmetic(value, 8), (8, COARSE))
+        place = spread_rows(jnp.bitwise_and(value, COARSE - 1), (COARSE, COARSE))
+        ones = jnp.where(place == iota_far, 1.0, 0.0).astype(BF16)
+        got = jnp.dot(cfw[...].reshape(3 * WIDTH, COARSE), ones, preferred_element_type=F32)
+        hits = [side == k for k in range(3)]
         for q in range(4):
             picked = jnp.zeros((8, COARSE), F32)
-            for k in range(6):
+            for k in range(3):
                 picked = jnp.where(hits[k], got[WIDTH * k + 8 * q : WIDTH * k + 8 * q + 8], picked)
             for c in range(2):
                 near[c, pl.ds(32 * 8 * q + j, 8, stride=32), :] = picked[:, LANES * c : LANES * (c + 1)]
@@ -296,7 +287,7 @@
                 kern[c, s0 + g, 8 * b : 8 * b + 8, :] = dots[g][b] * product[8 * b : 8 * b + 8]
         return carry
 
-    lax.fori_loop(0, 2 * SLOTS // group, kernel_values, 0)
+    lax.fori_loop(0, SLOTS // group, kernel_values, 0)
 
     arrive(near_by)
     xw1[0:8, :] = from_left[0:8, :] + to_left[0:8, :] + from_left[24:32, :]
@@ -305,7 +296,7 @@
     shift_s[...] = shift_s[...] + (from_left[16:24, :] + from_right[16:24, :])
     forward(xw1, False)
     q0 = xw1[8:16, :]
-    first = to_others(ag, gy, row_of(r0 * r0, r0 * q0, q0 * q0, shift_s[...] * (q0 * q0) + 2.0 * q0 * fwd[...]), ag_send, ag_recv, plane)
+    first = to_others(ag, gy, tile_of(r0 * r0, r0 * q0, q0 * q0, shift_s[...] * (q0 * q0) + 2.0 * q0 * fwd[...]), ag_send, ag_recv, plane)
     for r in range(ROWS):
         row1[0:1, LANES * r : LANES * (r + 1)] = q0[r : r + 1]
 
@@ -321,6 +312,8 @@
         copy.start()
 
     second = to_others(agx, gx, sum_of(ag, first), agx_send, agx_recv, column)
+
+    lax.fori_loop(SLOTS // group, 2 * SLOTS // group, kernel_values, 0)
 
     def gram_rows(i, carry):
         c = lax.rem(i, 2)
@@ -338,15 +331,18 @@
         return carry
 
     lax.fori_loop(0, 18, gram_rows, 0)
-    row = sum_of(agx, second)
-    rr0, rq, qq, qaq = [jnp.sum(jnp.where(lane_group == i, row, 0.0), axis=1, keepdims=True) for i in range(4)]
-    alpha0 = rr0 / rq
-    shear = rq / rr0
-    hh = qq - shear * rq
-    hah = qaq - 2.0 * shear * qq + shear * shear * rq
-    rr1 = alpha0 * alpha0 * hh
+    tile = sum_of(agx, second)
+    rr, rq, qq, qaq = [tile[i : i + 1] for i in range(4)]
+
+    def over_lanes(value):
+        return jnp.sum(value, axis=1, keepdims=True)
+
+    rr0 = over_lanes(rr)
+    alpha0 = rr0 / over_lanes(rq)
+    rr1 = over_lanes(rr - alpha0 * (2.0 * rq - alpha0 * qq))
+    rar1 = over_lanes(rq - alpha0 * (2.0 * qq - alpha0 * qaq))
     beta = rr1 / rr0
-    alpha1 = rr1 / (alpha0 * alpha0 * hah - beta * rr1 * shear)
+    alpha1 = rr1 / (rar1 - beta * rr1 / alpha0)
     arrive(ends)
     r1 = r0 - alpha0 * q0
     image = shift_s[...] * q0 + fwd[...] + (mid1[...] + from_left1[...] + from_right1[...])
@@ -408,10 +404,9 @@
             vm(fine, F32),
             vm(fine, F32),
             vm(fine, F32),
-            vm((n_gy, 1, LANES), F32),
-            vm((n_gx, 1, LANES), F32),
+            vm((n_gy, 4, LANES), F32),
+            vm((n_gx, 4, LANES), F32),
             vm((3, WIDTH, COARSE), BF16),
-            vm((6 * WIDTH, LANES), BF16),
             vm((WIDTH, POINTS), F32),
             vm((2, WIDTH * 32, LANES), F32),
             vm((2, SLOTS, 32, LANES), F32),

time: 29.5 us -> 29 us (0.983); the launches traced: 29 us -> 28.8 us
  Pallas kernels: 28.4 us -> 28.1 us
where the time goes in v4:
time: 29 us; the launch traced here: 28.8 us
  Pallas kernels  28.1 us (97%)
  between operations  0.64 us (2%)
    pallas_call x1, Pallas kernels, on_device(): pl.pallas_call(functools.partial(kernel, n_gx, n_gy), out_shape=[pltpu.VM...  27.4 us
    pallas_call x1, Pallas kernels, on_device(): pl.pallas_call(hand_over, out_shape=[jax.ShapeDtypeStruct(fine, F32), jax...  0.79 us

profile of v4, /device:TPU:1, one launch (start us, length us, event | category | flops | bytes accessed | tf_op | source)
XLA Modules:
  0.0 28.8 jit_solution(9999040581244974132)
XLA Ops:
  0.6 27.4 %shard_map.130 = (f32[8,128]{1,0:T(8,128)S(1)}, f32[8,128]{1,0:T(8,128)S(1)}, bf16[27,27,256]{2,1,0:T(8,128)(2,1)S(1)}) custom-call(f32[8,128]{1,0:T(8,128)} %bitcast.7, f32[1,1024]{1,0:T(1,128)} %bitcast.8, f32[8,128]{1,0:T(8,128)} %bitcast.10, s32[27,1024]{1,0:T(8,128)} %sup.1, f32[27,1024]{1,0:T(8,128)} %wts.1, bf16[32,4096]{1,0:T(8,128)(2,1)} %pin.1, ...), custom_call_target="tpu_custom_call" | custom-call | tf_op jit(solution)/shard_map/pallas_call | solution.py:368
  28.0 0.8 %shard_map.131 = (f32[8,128]{1,0:T(8,128)}, f32[8,128]{1,0:T(8,128)}, bf16[27,27,256]{2,1,0:T(8,128)(2,1)}) custom-call(f32[8,128]{1,0:T(8,128)S(1)} %get-tuple-element.9.sol, f32[8,128]{1,0:T(8,128)S(1)} %get-tuple-element.10.res, bf16[27,27,256]{2,1,0:T(8,128)(2,1)S(1)} %get-tuple-element.11.gram), custom_call_target="tpu_custom_call" | custom-call | tf_op jit(solution)/shard_map/pallas_call | solution.py:432

commit v5 on v4

--- a/solution.py
+++ b/solution.py
@@ -52,8 +52,15 @@
 
     left2, left, right, right2 = device(-2), device(-1), device(1), device(2)
 
-    plane = [(gx, lax.rem(gy + d, n_gy)) for d in range(1, n_gy)]
-    column = [(lax.rem(gx + d, n_gx), gy) for d in range(1, n_gx)]
+    def hops(count, inner):
+        def key(d):
+            outer, low = divmod(d, inner)
+            return -min(outer, count // inner - outer) - min(low, inner - low)
+
+        return sorted(range(1, count), key=key)
+
+    plane = [(gx, lax.rem(gy + d, n_gy)) for d in hops(n_gy, 4)]
+    column = [(lax.rem(gx + d, n_gx), gy) for d in hops(n_gx, 2)]
 
     moves = [
         (rhs, xw0.at[pl.ds(8, 8)]), (cf, cfw.at[1]), (sup, sup_v), (wts, wts_v), (rhs_row, row0), (diag, diag_v),
@@ -107,8 +114,8 @@
         started.extend(copies)
 
     halo0 = [
-        remote(xw0.at[pl.ds(8, 8)], xw0.at[pl.ds(0, 8)], halo_send.at[0], halo_recv.at[0], right),
-        remote(xw0.at[pl.ds(8, 8)], xw0.at[pl.ds(16, 8)], halo_send.at[1], halo_recv.at[1], left),
+        remote(rhs, xw0.at[pl.ds(0, 8)], halo_send.at[0], halo_recv.at[0], right),
+        remote(rhs, xw0.at[pl.ds(16, 8)], halo_send.at[1], halo_recv.at[1], left),
     ]
     for copy in halo0:
         copy.start()

time: 29 us -> 29 us (level)
  no operation moved by 1% of the time
where the time goes in v5:
time: 29 us; the launch traced here: 28.7 us
  Pallas kernels  28 us (97%)
  between operations  0.64 us (2%)
    pallas_call x1, Pallas kernels, on_device(): pl.pallas_call(functools.partial(kernel, n_gx, n_gy), out_shape=[pltpu.VM...  27.2 us
    pallas_call x1, Pallas kernels, on_device(): pl.pallas_call(hand_over, out_shape=[jax.ShapeDtypeStruct(fine, F32), jax...  0.79 us

profile of v5, /device:TPU:1, one launch (start us, length us, event | category | flops | bytes accessed | tf_op | source)
XLA Modules:
  0.0 28.7 jit_solution(15665808305654435403)
XLA Ops:
  0.6 27.2 %shard_map.130 = (f32[8,128]{1,0:T(8,128)S(1)}, f32[8,128]{1,0:T(8,128)S(1)}, bf16[27,27,256]{2,1,0:T(8,128)(2,1)S(1)}) custom-call(f32[8,128]{1,0:T(8,128)} %bitcast.7, f32[1,1024]{1,0:T(1,128)} %bitcast.8, f32[8,128]{1,0:T(8,128)} %bitcast.10, s32[27,1024]{1,0:T(8,128)} %sup.1, f32[27,1024]{1,0:T(8,128)} %wts.1, bf16[32,4096]{1,0:T(8,128)(2,1)} %pin.1, ...), custom_call_target="tpu_custom_call" | custom-call | tf_op jit(solution)/shard_map/pallas_call | solution.py:375
  27.9 0.8 %shard_map.131 = (f32[8,128]{1,0:T(8,128)}, f32[8,128]{1,0:T(8,128)}, bf16[27,27,256]{2,1,0:T(8,128)(2,1)}) custom-call(f32[8,128]{1,0:T(8,128)S(1)} %get-tuple-element.9.sol, f32[8,128]{1,0:T(8,128)S(1)} %get-tuple-element.10.res, bf16[27,27,256]{2,1,0:T(8,128)(2,1)S(1)} %get-tuple-element.11.gram), custom_call_target="tpu_custom_call" | custom-call | tf_op jit(solution)/shard_map/pallas_call | solution.py:439
